TPU v7x, 32 devices: a whole 2x2x4 slice. The times are simulated.
32 devices in a mesh: wide: 8 (over y, x, core), narrow: 4 (over z).
Axes of the slice: x: 2, y: 2, z: 4, core: 2. Of those that a mesh axis runs over, the one named last changes fastest.
Arguments:
- patches: bfloat16 [16384, 768], P('wide'), may hold values from -6 to 6
- mask_index: int32 [32, 450], P('wide'), may hold values from 0 to 511, as said below
- mask_count: int32 [32], P('wide'), may hold values from 100 to 450, as said below
- mask_embed: float32 [768], replicated, may hold values from -5 to 5
- norm1_gain: float32 [768], replicated, may hold values from 0.5 to 1.5
- norm1_bias: float32 [768], replicated, may hold values from -1 to 1
- w_qkv: bfloat16 [3, 768, 768], P(None, None, 'narrow'), may hold values from -0.21875 to 0.21875
- b_qv: float32 [2, 768], P(None, 'narrow'), may hold values from -1.5 to 1.5
- w_out: bfloat16 [768, 768], P('narrow'), may hold values from -1.75 to 1.75
- b_out: float32 [768], replicated, may hold values from -1 to 1
- norm2_gain: float32 [768], replicated, may hold values from 0.5 to 1.5
- norm2_bias: float32 [768], replicated, may hold values from -1 to 1
- w_up: bfloat16 [768, 3072], P(None, 'narrow'), may hold values from -0.21875 to 0.21875
- b_up: float32 [3072], P('narrow'), may hold values from -2.5 to 2.5
- w_down: bfloat16 [3072, 768], P('narrow'), may hold values from -0.625 to 0.625
- b_down: float32 [768], replicated, may hold values from -1 to 1
- cotangent: bfloat16 [16384, 768], P('wide'), may hold values from -6 to 6
Outputs:
- output: bfloat16 [16384, 768], P('wide')
- patch_grad: bfloat16 [16384, 768], P('wide')
- mask_embed_grad: float32 [768], replicated
- norm1_gain_grad: float32 [768], replicated
- norm1_bias_grad: float32 [768], replicated
- qkv_grad: float32 [3, 768, 768], P(None, None, 'narrow')
- qv_bias_grad: float32 [2, 768], P(None, 'narrow')
- out_grad: float32 [768, 768], P('narrow')
- out_bias_grad: float32 [768], replicated
- norm2_gain_grad: float32 [768], replicated
- norm2_bias_grad: float32 [768], replicated
- up_grad: float32 [768, 3072], P(None, 'narrow')
- up_bias_grad: float32 [3072], P('narrow')
- down_grad: float32 [3072, 768], P('narrow')
- down_bias_grad: float32 [768], replicated
Inputs may be any that keep to these rules, and one draw needn't show every extreme that they name: `mask_index`: the 450 entries of a clip are distinct patch positions; only the first mask_count of them are used. `mask_count`: in every draw one clip has exactly 450 masked patches and another exactly 100.
All inputs are finite; a program needn't handle non-finite values.
Results may differ from a plain program's by a relative error of at most 0.014.
The roundings to bfloat16 on the way count: a program that leaves them out, or rounds other values in their place, can miss the bound.
Values sent between devices are 32-bit elements; how exact they have to be, the bound alone decides.
A program may use at most 128 MiB of HBM per device.

v0:
```python
import math

import jax
import jax.numpy as jnp
from jax import lax
from jax.sharding import PartitionSpec as P

HD = 64
PATCHES = 512


epsilon = 1e-06


def masked_rows(mask_index, mask_count, length):
    slot_ids = jnp.arange(mask_index.shape[1], dtype=jnp.int32)
    in_use = slot_ids[None, :] < mask_count[:, None]
    position = jnp.arange(length, dtype=jnp.int32)
    matches = (mask_index[:, :, None] == position[None, None, :]) & in_use[:, :, None]
    return jnp.any(matches, axis=1)


def norm_forward(values, norm_gain, norm_shift):
    centred = values - jnp.mean(values, axis=-1, keepdims=True)
    inverse = lax.rsqrt(jnp.mean(centred * centred, axis=-1, keepdims=True) + epsilon)
    scaled = centred * inverse
    return ((scaled * norm_gain + norm_shift).astype(jnp.bfloat16), scaled, inverse)


def norm_backward(upstream, scaled, inverse, norm_gain):
    weighted = upstream * norm_gain
    centred_grad = (
        weighted
        - jnp.mean(weighted, axis=-1, keepdims=True)
        - scaled * jnp.mean(weighted * scaled, axis=-1, keepdims=True)
    )
    return (inverse * centred_grad, jnp.sum(upstream * scaled, axis=0), jnp.sum(upstream, axis=0))


def gelu_slope(values):
    return (
        0.5 * (1.0 + lax.erf(values * 0.5**0.5))
        + values * jnp.exp(-0.5 * values * values) * (0.5 / math.pi) ** 0.5
    )


def attend_clip(heads):
    query_heads, key_heads, value_heads = heads
    scaling = HD ** (-0.5)
    scores = (
        jnp.einsum("qhd,khd->hqk", query_heads, key_heads, preferred_element_type=jnp.float32)
        * scaling
    )
    highest = jnp.max(scores, axis=-1, keepdims=True)
    raised = jnp.exp(scores - highest)
    row_total = jnp.sum(raised, axis=-1, keepdims=True)
    attention = (raised / row_total).astype(jnp.bfloat16)
    context = jnp.einsum(
        "hqk,khd->qhd", attention, value_heads, preferred_element_type=jnp.float32
    ).astype(jnp.bfloat16)
    return (context, highest[..., 0] + jnp.log(row_total[..., 0]))


def attend_back(heads):
    query_heads, key_heads, value_heads, context_grad, log_total = heads
    scaling = HD ** (-0.5)
    scores = (
        jnp.einsum("qhd,khd->hqk", query_heads, key_heads, preferred_element_type=jnp.float32)
        * scaling
    )
    probs = jnp.exp(scores - log_total[..., None])
    value_grad = jnp.einsum(
        "hqk,qhd->khd", probs.astype(jnp.bfloat16), context_grad, preferred_element_type=jnp.float32
    )
    probs_grad = jnp.einsum(
        "qhd,khd->hqk", context_grad, value_heads, preferred_element_type=jnp.float32
    )
    scores_grad = (
        probs * (probs_grad - jnp.sum(probs * probs_grad, axis=-1, keepdims=True))
    ).astype(jnp.bfloat16)
    query_grad = (
        jnp.einsum("hqk,khd->qhd", scores_grad, key_heads, preferred_element_type=jnp.float32)
        * scaling
    ).astype(jnp.bfloat16)
    key_grad = (
        jnp.einsum("hqk,qhd->khd", scores_grad, query_heads, preferred_element_type=jnp.float32)
        * scaling
    ).astype(jnp.bfloat16)
    return (query_grad, key_grad, value_grad.astype(jnp.bfloat16))


def forward(replaced, weights):
    (
        norm1_gain,
        norm1_bias,
        w_qkv,
        qkv_shift,
        w_out,
        b_out,
        norm2_gain,
        norm2_bias,
        w_up,
        b_up,
        w_down,
        b_down,
    ) = weights
    row_count = replaced.shape[0]
    clip_count = row_count // PATCHES
    local_heads = w_qkv.shape[2] // HD
    normed, scaled1, inverse1 = norm_forward(replaced, norm1_gain, norm1_bias)
    projected = jnp.einsum("td,jde->jte", normed, w_qkv, preferred_element_type=jnp.float32)
    projected = (projected + qkv_shift[:, None, :]).astype(jnp.bfloat16)
    qkv_heads = projected.reshape(3, clip_count, PATCHES, local_heads, HD)
    context, log_total = lax.map(attend_clip, (qkv_heads[0], qkv_heads[1], qkv_heads[2]))
    attention_part = jnp.dot(
        context.reshape(row_count, -1), w_out, preferred_element_type=jnp.float32
    )
    middle = replaced + lax.psum(attention_part, "narrow") + b_out
    hidden_in, scaled2, inverse2 = norm_forward(middle, norm2_gain, norm2_bias)
    before = jnp.dot(hidden_in, w_up, preferred_element_type=jnp.float32) + b_up
    active = jax.nn.gelu(before, approximate=False).astype(jnp.bfloat16)
    down_part = jnp.dot(active, w_down, preferred_element_type=jnp.float32)
    result = middle + lax.psum(down_part, "narrow") + b_down
    stored = (
        normed,
        scaled1,
        inverse1,
        qkv_heads,
        context,
        log_total,
        hidden_in,
        scaled2,
        inverse2,
        before,
        active,
    )
    return (result, stored)


def on_device(
    patches,
    mask_index,
    mask_count,
    mask_embed,
    norm1_gain,
    norm1_bias,
    w_qkv,
    b_qv,
    w_out,
    b_out,
    norm2_gain,
    norm2_bias,
    w_up,
    b_up,
    w_down,
    b_down,
    cotangent,
):
    masked = masked_rows(mask_index, mask_count, PATCHES).reshape(-1, 1)
    replaced = jnp.where(masked, mask_embed[None, :], patches.astype(jnp.float32))
    qkv_shift = jnp.stack([b_qv[0], jnp.zeros_like(b_qv[0]), b_qv[1]])
    weights = (
        norm1_gain,
        norm1_bias,
        w_qkv,
        qkv_shift,
        w_out,
        b_out,
        norm2_gain,
        norm2_bias,
        w_up,
        b_up,
        w_down,
        b_down,
    )
    result, stored = forward(replaced, weights)
    output = result.astype(jnp.bfloat16)
    fenced = lax.optimization_barrier((replaced, output))
    stored = forward(fenced[0], weights)[1]
    (
        normed,
        scaled1,
        inverse1,
        qkv_heads,
        context,
        log_total,
        hidden_in,
        scaled2,
        inverse2,
        before,
        active,
    ) = stored
    row_count = replaced.shape[0]
    out_grad_rows = cotangent.astype(jnp.float32)
    down_bias_grad = jnp.sum(out_grad_rows, axis=0)
    down_grad = jnp.einsum("tf,td->fd", active, cotangent, preferred_element_type=jnp.float32)
    active_grad = jnp.einsum("td,fd->tf", cotangent, w_down, preferred_element_type=jnp.float32)
    before_grad = (active_grad * gelu_slope(before)).astype(jnp.bfloat16)
    up_bias_grad = jnp.sum(before_grad, axis=0, dtype=jnp.float32)
    up_grad = jnp.einsum("td,tf->df", hidden_in, before_grad, preferred_element_type=jnp.float32)
    hidden_part = jnp.einsum("tf,df->td", before_grad, w_up, preferred_element_type=jnp.float32)
    hidden_grad = lax.psum(hidden_part, "narrow")
    middle_part, norm2_gain_grad, norm2_bias_grad = norm_backward(
        hidden_grad, scaled2, inverse2, norm2_gain
    )
    middle_grad = out_grad_rows + middle_part
    out_bias_grad = jnp.sum(middle_grad, axis=0)
    middle_low = middle_grad.astype(jnp.bfloat16)
    out_weight_grad = jnp.einsum(
        "te,td->ed", context.reshape(row_count, -1), middle_low, preferred_element_type=jnp.float32
    )
    context_grad = jnp.einsum(
        "td,ed->te", middle_low, w_out, preferred_element_type=jnp.float32
    ).astype(jnp.bfloat16)
    head_grads = lax.map(
        attend_back,
        (qkv_heads[0], qkv_heads[1], qkv_heads[2], context_grad.reshape(context.shape), log_total),
    )
    qkv_grad_rows = jnp.stack(head_grads).reshape(3, row_count, -1)
    qkv_weight_grad = jnp.einsum(
        "td,jte->jde", normed, qkv_grad_rows, preferred_element_type=jnp.float32
    )
    qv_bias_grad = jnp.stack(
        [
            jnp.sum(qkv_grad_rows[0], axis=0, dtype=jnp.float32),
            jnp.sum(qkv_grad_rows[2], axis=0, dtype=jnp.float32),
        ]
    )
    normed_part = jnp.einsum(
        "jte,jde->td", qkv_grad_rows, w_qkv, preferred_element_type=jnp.float32
    )
    normed_grad = lax.psum(normed_part, "narrow")
    replaced_part, norm1_gain_grad, norm1_bias_grad = norm_backward(
        normed_grad, scaled1, inverse1, norm1_gain
    )
    replaced_grad = middle_grad + replaced_part
    embed_grad = jnp.sum(jnp.where(masked, replaced_grad, 0.0), axis=0)
    patch_grad = jnp.where(masked, 0.0, replaced_grad).astype(jnp.bfloat16)
    totals = tuple(
        lax.psum(
            (
                embed_grad,
                norm1_gain_grad,
                norm1_bias_grad,
                qkv_weight_grad,
                qv_bias_grad,
                out_weight_grad,
                out_bias_grad,
                norm2_gain_grad,
                norm2_bias_grad,
                up_grad,
                up_bias_grad,
                down_grad,
                down_bias_grad,
            ),
            "wide",
        )
    )
    return (output, patch_grad) + totals


def solution(mesh):
    return jax.shard_map(
        on_device,
        mesh=mesh,
        in_specs=(
            P("wide", None),
            P("wide", None),
            P("wide"),
            P(),
            P(),
            P(),
            P(None, None, "narrow"),
            P(None, "narrow"),
            P("narrow", None),
            P(),
            P(),
            P(),
            P(None, "narrow"),
            P("narrow"),
            P("narrow", None),
            P(),
            P("wide", None),
        ),
        out_specs=(
            P("wide", None),
            P("wide", None),
            P(),
            P(),
            P(),
            P(None, None, "narrow"),
            P(None, "narrow"),
            P("narrow", None),
            P(),
            P(),
            P(),
            P(None, "narrow"),
            P("narrow"),
            P("narrow", None),
            P(),
        ),
        check_vma=False,
    )
```

profile of v0, /device:TPU:0, one launch (start us, length us, event | category | flops | bytes accessed | tf_op | source)
XLA Modules:
  0.0 1476.2 jit_solution(2927989340911728786)
XLA Ops:
  26.8 24.7 %while.36 = (s32[]{:T(128)}, bf16[4,512,3,64]{1,3,2,0:T(8,128)(2,1)S(1)}, bf16[4,512,3,64]{1,3,2,0:T(8,128)(2,1)S(1)}, bf16[4,512,3,64]{1,3,2,0:T(8,128)(2,1)}, bf16[4,512,3,64]{1,3,2,0:T(8,128)(2,1)}, /*index=5*/s32[]{:T(128)}) while((s32[]{:T(128)}, bf16[4,512,3,64]{1,3,2,0:T(8,128)(2,1)S(1)}, bf16[4,512,3,64]{1,3,2,0:T(8,128)(2,1)S(1)}, ...), condition=%wide.region_6.7_spmd, body=%wide.region_3.6_spmd.sunk | while | flops 205357568 | bytes 7094349 | solution.py:114
  26.8 3.9 fusion.277
  33.0 3.9 fusion.277
  39.2 3.9 fusion.277
  45.3 3.9 fusion.277
  52.3 3.7 fusion.223
  56.4 225.4 %all-reduce.9.cloned.1.call-done = f32[2048,768]{1,0:T(8,128)} async-done(((f32[2048,768]{1,0:T(8,128)}), f32[2048,768]{1,0:T(8,128)}) %all-reduce.9.cloned.1.call-update) | async-done | bytes 6291472 | tf_op jit(solution)/shard_map/psum | solution.py:118
  281.8 5.0 fusion.208
  288.3 3.7 convert_select_fusion
  292.0 22.5 %fusion.141 = f32[2048,768]{1,0:T(8,128)} fusion(bf16[768,768]{1,0:T(8,128)(2,1)S(1)} %copy-done.46, bf16[768,768]{1,0:T(8,128)(2,1)S(1)} %copy-done, f32[768]{0:T(1024)S(1)} %copy-done.50, f32[768]{0:T(1024)S(1)} %copy-done.43, f32[768]{0:T(1024)S(1)} %copy-done.33, f32[2048]{0:T(1024)S(1)} %add_rsqrt_fusion.2, f32[2048]{0:T(1024)S(1)} %broadcast_multiply_fusion.6, ...), kind=kOutput, calls=%fused_computation.181 | convolution fusion | flops 4949803008 | bytes 18121728 | tf_op jit(solution)/shard_map/dot_general | solution.py:122
  314.6 12.0 all-reduce.13.cloned.1.call-start
  326.6 210.0 %all-reduce.11.cloned.1.call-done = f32[2048,768]{1,0:T(8,128)} async-done(((f32[2048,768]{1,0:T(8,128)}), f32[2048,768]{1,0:T(8,128)}) %all-reduce.11.cloned.1.call-update) | async-done | bytes 6291472 | tf_op jit(solution)/shard_map/psum | solution.py:123
  536.6 8.0 add_convert_fusion.2
  547.8 3.6 multiply_reduce_fusion.8
  566.8 12.9 while.37
  582.8 4.6 fusion.225
  587.5 221.9 %all-reduce.13.cloned.1.call-done = f32[2048,768]{1,0:T(8,128)} async-done(((f32[2048,768]{1,0:T(8,128)}), f32[2048,768]{1,0:T(8,128)}) %all-reduce.13.cloned.1.call-update) | async-done | bytes 6291472 | tf_op jit(solution)/shard_map/psum | solution.py:118
  809.4 5.4 fusion.210
  820.8 6.2 convert_reduce_fusion.1
  828.7 4.6 fusion.227
  833.8 221.5 %all-reduce.15.cloned.1.call-done = f32[2048,768]{1,0:T(8,128)} async-done(((f32[2048,768]{1,0:T(8,128)}), f32[2048,768]{1,0:T(8,128)}) %all-reduce.15.cloned.1.call-update) | async-done | bytes 6291472 | tf_op jit(solution)/shard_map/psum | solution.py:202
  1055.4 6.6 multiply_reduce_fusion.3
  1062.7 5.3 fusion.209
  1074.6 27.8 %while.38 = (s32[]{:T(128)}, bf16[4,512,3,64]{1,3,2,0:T(8,128)(2,1)}, bf16[4,512,3,64]{1,3,2,0:T(8,128)(2,1)}, bf16[4,512,3,64]{1,3,2,0:T(8,128)(2,1)S(1)}, bf16...) while((s32[]{:T(128)}, ...), condition=%wide.region_25.26_spmd, body=%wide.region_23.25_spmd.sunk | while | flops 513243648 | bytes 25611376 | solution.py:215
  1115.3 6.0 convolution_bitcast_fusion
  1121.5 7.1 fusion.228
  1128.5 17.8 %fusion.137 = f32[768,768]{1,0:T(8,128)} fusion(bf16[2048,768]{1,0:T(8,128)(2,1)S(1)} %copy-done.18, f32[2048,768]{1,0:T(8,128)} %copy-done.53, f32[768]{0:T(1024)S(1)} %copy-done.51), kind=kOutput, calls=%fused_computation.177 | convolution fusion | flops 2519728128 | bytes 11799552 | tf_op jit(solution)/shard_map/tf,td->fd/dot_general | solution.py:196
  1153.1 190.2 %all-reduce.17.cloned.1.call-done = f32[2048,768]{1,0:T(8,128)} async-done(((f32[2048,768]{1,0:T(8,128)}), f32[2048,768]{1,0:T(8,128)}) %all-reduce.17.cloned.1.call-update) | async-done | bytes 6291472 | tf_op jit(solution)/shard_map/psum | solution.py:232
  1343.3 6.0 multiply_reduce_fusion.4
  1349.8 8.1 select_reduce_fusion
  1357.8 27.9 %all-reduce = (f32[768]{0:T(1024)}, f32[768]{0:T(1024)}, f32[768]{0:T(1024)}, f32[2,192]{1,0:T(2,128)}, f32[768]{0:T(1024)}, /*index=5*/f32[768]{0:T(1024)}, f32[768]{0:T(1024)}, f32[768]{0:T(1024)}, f32[768]{0:T(1024)}) all-reduce(f32[768]{0:T(1024)S(1)} %get-tuple-element.255, ...), channel_id=1, replica_groups=mesh['wide'=8,'narrow'=4] {'wide'}, use_global_device_ids=true, to_apply=%region_30.31 | all-reduce | flops 6528 | bytes 52224 | tf_op jit(solution)/shard_map/psum | solution.py:240
  1389.1 72.4 %all-reduce.19.cloned.1.call-done = (f32[3,768,192]{1,2,0:T(8,128)}, f32[192,768]{1,0:T(8,128)}, f32[768,768]{1,0:T(8,128)}, f32[768,768]{1,0:T(8,128)}) async-done(((f32[3,768,192]{1,2,0:T(8,128)}, f32[192,768]{1,0:T(8,128)}, f32[768,768]{1,0:T(8,128)}, f32[768,768]{1,0:T(8,128)}), (f32[3,768,192]{1,2,0:T(8,128)}, f32[192,768]{1,0:T(8,128)}, f32[768,768]{1,0:T(8,128)}, ...) | async-done | bytes 7077904 | tf_op jit(solution)/shard_map/psum | solution.py:240
  (249 shorter events, 140.0 us)
Async XLA Ops:
  7.2 284.8 %copy-start = (bf16[768,768]{1,0:T(8,128)(2,1)S(1)}, bf16[768,768]{1,0:T(8,128)(2,1)}, u32[]{:S(2)}) copy-start(bf16[768,768]{1,0:T(8,128)(2,1)} %param.35) | copy-start | bytes 3538948
  7.2 10.3 copy-start.31
  7.2 10.3 copy-start.35
  7.2 10.3 copy-start.48
  7.2 10.3 copy-start.41
  7.2 274.5 %all-reduce.9.cloned.1.call-start = ((), (), s32[]{:S(2)}) async-start(), calls=%async_computation | async-start | bytes 12582912 | tf_op jit(solution)/shard_map/psum | solution.py:118
  9.7 7.9 copy-start.4
  11.7 524.9 %copy-start.29 = (pred[1,4,4,128]{3,1,2,0:T(4,128)(4,1)}, pred[1,4,4,128]{3,1,2,0:T(4,128)(4,1)S(1)}, u32[]{:S(2)}) copy-start(pred[1,4,4,128]{3,1,2,0:T(4,128)(4,1)S(1)} %copy.96) | copy-start | bytes 6148
  26.7 25.6 %copy-start.19 = (bf16[192,768]{1,0:T(8,128)(2,1)S(1)}, bf16[192,768]{1,0:T(8,128)(2,1)}, u32[]{:S(2)}) copy-start(bf16[192,768]{1,0:T(8,128)(2,1)} %param.31) | copy-start | bytes 884740
  52.3 229.5 %copy-start.32 = (f32[768]{0:T(1024)S(1)}, f32[768]{0:T(1024)}, u32[]{:S(2)}) copy-start(f32[768]{0:T(1024)} %param.32) | copy-start | bytes 9220
  56.1 480.5 %all-reduce.11.cloned.1.call-start = ((), (), s32[]{:S(2)}) async-start(), calls=%async_computation.1 | async-start | bytes 12582912 | tf_op jit(solution)/shard_map/psum | solution.py:123
  314.6 222.0 %copy-start.40 = (f32[768]{0:T(1024)S(1)}, f32[768]{0:T(1024)}, u32[]{:S(2)}) copy-start(f32[768]{0:T(1024)} %param.38) | copy-start | bytes 9220
  314.6 494.8 %all-reduce.13.cloned.1.call-start = ((), (), s32[]{:S(2)}) async-start(), calls=%async_computation.2 | async-start | bytes 12582912 | tf_op jit(solution)/shard_map/psum | solution.py:118
  547.8 7.1 copy-start.25
  579.7 7.7 copy-start.12
  587.4 467.9 %all-reduce.15.cloned.1.call-start = ((), (), s32[]{:S(2)}) async-start(), calls=%async_computation.3 | async-start | bytes 12582912 | tf_op jit(solution)/shard_map/psum | solution.py:202
  833.4 509.9 %all-reduce.17.cloned.1.call-start = ((), (), s32[]{:S(2)}) async-start(), calls=%async_computation.4 | async-start | bytes 12582912 | tf_op jit(solution)/shard_map/psum | solution.py:232
  1055.4 7.4 copy-start.17
  1062.7 7.9 copy-start.20
  1121.4 340.1 %all-reduce.19.cloned.1.call-start = ((), (), s32[]{:S(2)}) async-start(), calls=%async_computation.5 | async-start | bytes 14155776 | tf_op jit(solution)/shard_map/psum | solution.py:240
  1121.4 7.1 copy-start.18
  1121.5 24.9 %slice-start = ((s8[6291456]{0:T(1024)(128)(4,1)}), s8[4194304]{0:T(1024)(128)(4,1)S(1)}, s32[]{:S(2)}) async-start(s8[6291456]{0:T(1024)(128)(4,1)} %bitcast.218), calls=%async_computation.6 | async-start | bytes 8388608
  1128.5 17.8 %slice-start.1 = ((s8[6291456]{0:T(1024)(128)(4,1)}), s8[2097152]{0:T(1024)(128)(4,1)S(1)}, s32[]{:S(2)}) async-start(s8[6291456]{0:T(1024)(128)(4,1)} %bitcast.218), calls=%async_computation.7 | async-start | bytes 4194304
  1128.5 17.8 %copy-start.10 = (bf16[24,8,4,512]{3,1,2,0:T(8,128)(2,1)S(1)}, bf16[24,8,4,512]{3,1,2,0:T(8,128)(2,1)}, u32[]{:S(2)}) copy-start(bf16[24,8,4,512]{3,1,2,0:T(8,128)(2,1)} %copy-done.9) | copy-start | bytes 2359300
  1152.5 190.8 %copy-start.26 = (f32[2048]{0:T(1024)S(1)}, f32[2048]{0:T(1024)}, u32[]{:S(2)}) copy-start(f32[2048]{0:T(1024)} %copy-done.25) | copy-start | bytes 24580
  1152.5 190.8 %copy-start.28 = (f32[2048]{0:T(1024)S(1)}, f32[2048]{0:T(1024)}, u32[]{:S(2)}) copy-start(f32[2048]{0:T(1024)} %copy-done.27) | copy-start | bytes 24580
  1152.5 190.8 %copy-start.37 = (f32[768]{0:T(1024)S(1)}, f32[768]{0:T(1024)}, u32[]{:S(2)}) copy-start(f32[768]{0:T(1024)} %param.27) | copy-start | bytes 9220
  1153.1 196.3 %copy-start.30 = (pred[1,4,4,128]{3,1,2,0:T(4,128)(4,1)S(1)}, pred[1,4,4,128]{3,1,2,0:T(4,128)(4,1)}, u32[]{:S(2)}) copy-start(pred[1,4,4,128]{3,1,2,0:T(4,128)(4,1)} %copy-done.29) | copy-start | bytes 6148
  1349.7 8.1 copy-start.38
  1349.7 8.1 copy-start.39
  1349.8 8.1 copy-start.45
  1461.5 7.7 copy-start.1
  (30 other events, 116.5 us)
Sparse Core Ops, SparseCore 0:
  56.2 225.5 all-reduce.8
  314.7 221.7 all-reduce.10
  587.6 221.7 all-reduce.12
  833.5 221.7 all-reduce.14
  1121.5 221.7 all-reduce.16
  1348.0 113.4 all-reduce.18
where the time goes:
time: 1490 us; the launch traced here: 1480 us
  waiting for transfers between devices  1140 us (77%)
  matrix products  140 us (9%)
  other arithmetic  81.1 us (5%)
  local copies, waits for them, and re-layouts  57.2 us (4%)
  blocking collectives  27.9 us (2%)
  between operations  15.1 us (1%)
    psum x2, waiting for transfers between devices, forward(): middle = replaced + lax.psum(attention_part, 'narrow') + b_out  447 us
    psum x1, waiting for transfers between devices, on_device(): hidden_grad = lax.psum(hidden_part, 'narrow')  222 us
    psum x1, waiting for transfers between devices, forward(): result = middle + lax.psum(down_part, 'narrow') + b_down  210 us
    psum x1, waiting for transfers between devices, on_device(): normed_grad = lax.psum(normed_part, 'narrow')  190 us
    psum x1, waiting for transfers between devices, on_device(): lax.psum((embed_grad, norm1_gain_grad, norm1_bias_grad, qkv_weight_grad,...  72.4 us
  transfers between devices with their start and end apart: 6, of which 6 were waited for; matrix products, arithmetic and copies ran while one was open for 3% of the time, Pallas kernels for 0%

commit v1 on v0

v1 whole, which is shorter than its diff:
```python
import math

import jax
import jax.numpy as jnp
from jax import lax
from jax.sharding import PartitionSpec as P

HD = 64
PATCHES = 512
epsilon = 1e-06
f32 = jnp.float32
bf16 = jnp.bfloat16


def masked_rows(mask_index, mask_count, length):
    slot_ids = jnp.arange(mask_index.shape[1], dtype=jnp.int32)
    in_use = slot_ids[None, :] < mask_count[:, None]
    position = jnp.arange(length, dtype=jnp.int32)
    matches = (mask_index[:, :, None] == position[None, None, :]) & in_use[:, :, None]
    return jnp.any(matches, axis=1)


def norm_forward(values, norm_gain, norm_shift):
    centred = values - jnp.mean(values, axis=-1, keepdims=True)
    inverse = lax.rsqrt(jnp.mean(centred * centred, axis=-1, keepdims=True) + epsilon)
    scaled = centred * inverse
    return ((scaled * norm_gain + norm_shift).astype(bf16), scaled, inverse)


def norm_backward(upstream, scaled, inverse, norm_gain):
    weighted = upstream * norm_gain
    centred_grad = (
        weighted
        - jnp.mean(weighted, axis=-1, keepdims=True)
        - scaled * jnp.mean(weighted * scaled, axis=-1, keepdims=True)
    )
    return (inverse * centred_grad, jnp.sum(upstream * scaled, axis=0), jnp.sum(upstream, axis=0))


def gelu_parts(values):
    cdf = 0.5 * (1.0 + lax.erf(values * 0.5**0.5))
    slope = cdf + values * jnp.exp(-0.5 * values * values) * (0.5 / math.pi) ** 0.5
    return values * cdf, slope


def mm(spec, a, b):
    return jnp.einsum(spec, a, b, preferred_element_type=f32)


def make(mesh):
    nw, nz = mesh.shape["wide"], mesh.shape["narrow"]

    def on_device(
        patches, mask_index, mask_count, mask_embed, norm1_gain, norm1_bias, w_qkv, b_qv, w_out, b_out,
        norm2_gain, norm2_bias, w_up, b_up, w_down, b_down, cotangent,
    ):
        w, z = lax.axis_index("wide"), lax.axis_index("narrow")
        rows, d = patches.shape
        own = rows // nz
        hs = w_qkv.shape[2]
        fs = w_up.shape[1]
        qkv_t = jnp.swapaxes(w_qkv, 1, 2).reshape(3 * hs, d)
        pieces = (qkv_t, w_out, w_up, w_down)
        one = jnp.where(mask_count[0] >= 0, 1.0, 2.0).astype(f32)
        full = []
        for piece in pieces:
            n = piece.shape[0] // nw
            part = lax.dynamic_slice_in_dim(piece, w * n, n, 0).astype(f32)
            got = lax.all_gather(part, ("narrow", "wide"), axis=0, tiled=True)
            full.append((got * one).reshape((nz,) + piece.shape).astype(bf16))
        wq = full[0].reshape(nz, 3, hs, d).transpose(1, 0, 2, 3).reshape(3, nz * hs, d)
        wo = full[1].reshape(nz * hs, d)
        wu, wd = full[2], full[3]
        bq = lax.all_gather(b_qv, "narrow", axis=1, tiled=True)
        bu = lax.all_gather(b_up, "narrow", axis=0, tiled=False)
        heads = nz * hs // HD

        clip = lambda a: lax.dynamic_slice_in_dim(a, z * own, own, 0)
        masked = clip(masked_rows(mask_index, mask_count, PATCHES).reshape(-1, 1))
        rep = jnp.where(masked, mask_embed[None, :], clip(patches).astype(f32))
        cot = clip(cotangent)
        normed, xh1, r1 = norm_forward(rep, norm1_gain, norm1_bias)
        qkv = mm("td,jed->jte", normed, wq)
        qkv = qkv + jnp.stack([bq[0], jnp.zeros_like(bq[0]), bq[1]])[:, None, :]
        qkv = qkv.astype(bf16).reshape(3, own, heads, HD)
        q, k, v = qkv[0], qkv[1], qkv[2]
        scores = mm("qhd,khd->hqk", q, k) * HD**-0.5
        probs = jax.nn.softmax(scores, axis=-1)
        att = probs.astype(bf16)
        ctx = mm("hqk,khd->qhd", att, v).astype(bf16).reshape(own, -1)
        middle = rep + mm("te,ed->td", ctx, wo) + b_out
        hid, xh2, r2 = norm_forward(middle, norm2_gain, norm2_bias)
        before = mm("td,zdf->ztf", hid, wu) + bu[:, None, :]
        act, slope = gelu_parts(before)
        act = act.astype(bf16)
        out = middle + mm("ztf,zfd->td", act, wd) + b_down
        cf = cot.astype(f32)
        down_g = mm("ztf,td->zfd", act, cot)
        bg = (mm("td,zfd->ztf", cot, wd) * slope).astype(bf16)
        up_g = mm("td,ztf->zdf", hid, bg)
        up_bias = jnp.sum(bg, axis=1, dtype=f32)
        hg = mm("ztf,zdf->td", bg, wu)
        mp, g2, b2 = norm_backward(hg, xh2, r2, norm2_gain)
        mg = cf + mp
        ml = mg.astype(bf16)
        out_g = mm("te,td->ed", ctx, ml)
        cg = mm("td,ed->te", ml, wo).astype(bf16).reshape(own, heads, HD)
        vg = mm("hqk,qhd->khd", att, cg).astype(bf16)
        pg = mm("qhd,khd->hqk", cg, v)
        sg = (probs * (pg - jnp.sum(probs * pg, axis=-1, keepdims=True))).astype(bf16)
        qg = (mm("hqk,khd->qhd", sg, k) * HD**-0.5).astype(bf16)
        kg = (mm("hqk,qhd->khd", sg, q) * HD**-0.5).astype(bf16)
        grads = jnp.stack([qg, kg, vg]).reshape(3, own, -1)
        qkv_g = mm("jte,td->jed", grads, normed)
        qv_bias = jnp.stack([jnp.sum(grads[0], axis=0, dtype=f32), jnp.sum(grads[2], axis=0, dtype=f32)])
        ng = mm("jte,jed->td", grads, wq)
        rp, g1, b1 = norm_backward(ng, xh1, r1, norm1_gain)
        rg = mg + rp
        embed = jnp.sum(jnp.where(masked, rg, 0.0), axis=0)
        pgr = jnp.where(masked, 0.0, rg)

        def rows_out(a):
            got = lax.all_gather(a, "narrow", axis=0, tiled=True)
            return (got * one).astype(bf16)

        output = rows_out(out)
        patch_grad = rows_out(pgr)

        def weight_out(a):
            nzz, n, dd = a.shape
            r = lax.psum_scatter(
                a.reshape(nzz, nw, n // nw, dd), "wide", scatter_dimension=1, tiled=True
            )
            r = lax.psum_scatter(r, "narrow", scatter_dimension=0, tiled=True)
            return lax.all_gather(r.reshape(n // nw, dd), "wide", axis=0, tiled=True)

        down_o = weight_out(down_g)
        up_o = weight_out(up_g)
        out_o = weight_out(out_g.reshape(nz, hs, d))
        qkv_o = weight_out(
            qkv_g.reshape(3, nz, hs, d).transpose(1, 0, 2, 3).reshape(nz, 3 * hs, d)
        )
        qkv_o = jnp.swapaxes(qkv_o.reshape(3, hs, d), 1, 2)
        small = jnp.concatenate(
            [jnp.stack([embed, g1, b1, jnp.sum(mg, axis=0), g2, b2, jnp.sum(cf, axis=0)]), qv_bias, up_bias.reshape(-1, d)]
        )
        small = lax.psum(small, ("wide", "narrow"))
        qvb = lax.dynamic_slice_in_dim(small[7:9], z * hs, hs, 1)
        upb = lax.dynamic_slice_in_dim(small[9:].reshape(-1), z * fs, fs, 0)
        return (
            output, patch_grad, small[0], small[1], small[2], qkv_o, qvb, out_o, small[3],
            small[4], small[5], up_o, upb, down_o, small[6],
        )

    return on_device


def solution(mesh):
    return jax.shard_map(
        make(mesh),
        mesh=mesh,
        in_specs=(
            P("wide", None), P("wide", None), P("wide"), P(), P(), P(), P(None, None, "narrow"), P(None, "narrow"),
            P("narrow", None), P(), P(), P(), P(None, "narrow"), P("narrow"), P("narrow", None), P(), P("wide", None),
        ),
        out_specs=(
            P("wide", None), P("wide", None), P(), P(), P(), P(None, None, "narrow"), P(None, "narrow"),
            P("narrow", None), P(), P(), P(), P(None, "narrow"), P("narrow"), P("narrow", None), P(),
        ),
        check_vma=False,
    )
```

time: 1490 us -> 1200 us (0.81)
  waiting for transfers between devices: 1140 us -> 925 us
  matrix products: 140 us -> 82.4 us
  blocking collectives: 27.9 us -> 79.8 us
  other arithmetic: 81.1 us -> 46.9 us
  local copies, waits for them, and re-layouts: 57.2 us -> 39.7 us
    psum x6 -> x0, waiting for transfers between devices: 1140 us -> none  [the longest x2 447 us: forward(): middle = replaced + lax.psum(attention_part, 'narrow') + b_out]
    all_gather x0 -> x9, waiting for transfers between devices: none -> 506 us  [the longest x4 245 us: on_device(): got = lax.all_gather(part, ('narrow', 'wide'), axis=0, tiled=True)]
    unnamed x6 -> x15, waiting for transfers between devices: 0.1 us -> 341 us
    reduce_scatter x0 -> x4, waiting for transfers between devices: none -> 77.8 us  [weight_out(): r = lax.psum_scatter(r, 'narrow', scatter_dimension=0, tiled=True)]
    dot_general x44 -> x17, matrix products: 120 us -> 75.4 us  [mm(): return jnp.einsum(spec, a, b, preferred_element_type=f32)]
    all_gather x0 -> x3, blocking collectives: none -> 37.1 us  [the longest x1 13.7 us: on_device(): bq = lax.all_gather(b_qv, 'narrow', axis=1, tiled=True)]
    reduce_sum x10 -> x2, other arithmetic: 28.5 us -> 4.19 us  [the longest x1 2.29 us: on_device(): jnp.sum(mg, axis=0)]
    convert_element_type x10 -> x9, other arithmetic: 20.1 us -> 33.9 us  [the longest x2 10.8 us: on_device(): full.append((got * one).reshape((nz,) + piece.shape).astype(bf16))]
  transfers between devices with their start and end apart: 6 -> 14, of which waited for: 6 -> 14; matrix products, arithmetic and copies ran while one was open for 3% -> 6% of each run, Pallas kernels for 0% -> 0%
where the time goes in v1:
time: 1200 us; the launch traced here: 1190 us
  waiting for transfers between devices  925 us (77%)
  matrix products  82.4 us (7%)
  blocking collectives  79.8 us (7%)
  other arithmetic  46.9 us (4%)
  local copies, waits for them, and re-layouts  39.7 us (3%)
  between operations  15 us (1%)
    unnamed x15, waiting for transfers between devices  341 us
    all_gather x4, waiting for transfers between devices, on_device(): got = lax.all_gather(part, ('narrow', 'wide'), axis=0, tiled=True)  245 us
    all_gather x2, waiting for transfers between devices, rows_out(): got = lax.all_gather(a, 'narrow', axis=0, tiled=True)  183 us
    all_gather x3, waiting for transfers between devices, weight_out(): return lax.all_gather(r.reshape(n // nw, dd), 'wide', axis=0, tiled=True)  78 us
    reduce_scatter x4, waiting for transfers between devices, weight_out(): r = lax.psum_scatter(r, 'narrow', scatter_dimension=0, tiled=True)  77.8 us
    dot_general x17, matrix products, mm(): return jnp.einsum(spec, a, b, preferred_element_type=f32)  75.4 us
    psum x1, blocking collectives, on_device(): small = lax.psum(small, ('wide', 'narrow'))  42.7 us
  transfers between devices with their start and end apart: 14, of which 14 were waited for; matrix products, arithmetic and copies ran while one was open for 6% of the time, Pallas kernels for 0%

profile of v1, /device:TPU:0, one launch (start us, length us, event | category | flops | bytes accessed | tf_op | source)
XLA Modules:
  0.0 1189.9 jit_solution(15786558405989009163)
XLA Ops:
  14.0 13.7 %all-gather.5 = f32[4,192,2]{1,2,0:T(2,128)S(1)} all-gather(f32[1,192,2]{1,2,0:T(2,128)} %bitcast.218), channel_id=1, replica_groups=mesh['wide'=8,'narrow'=4] {'narrow'}, dimensions={0}, use_global_device_ids=true | all-gather | bytes 7680 | tf_op jit(solution)/shard_map/all_gather | solution.py:74
  30.8 13.2 %all-gather.6 = f32[4,1,768]{2,1,0:T(1,128)S(1)} all-gather(f32[1,1,768]{2,1,0:T(1,128)S(1)} %reshape.208), channel_id=2, replica_groups=mesh['wide'=8,'narrow'=4] {'narrow'}, dimensions={0}, use_global_device_ids=true | all-gather | bytes 15360 | tf_op jit(solution)/shard_map/all_gather | solution.py:75
  46.2 40.5 %all-gather.17.cloned.1.call-done = f32[2304,768]{1,0:T(8,128)} async-done(((f32[72,768]{1,0:T(8,128)}), f32[2304,768]{1,0:T(8,128)}) %all-gather.17.cloned.1.call-update) | async-done | bytes 7077904 | tf_op jit(solution)/shard_map/all_gather | solution.py:69
  93.6 7.0 fusion.63
  100.6 5.8 fusion.30
  106.4 39.6 %all-gather.19.cloned.1.call-done = f32[768,768]{1,0:T(8,128)} async-done(((f32[24,768]{1,0:T(8,128)}), f32[768,768]{1,0:T(8,128)}) %all-gather.19.cloned.1.call-update) | async-done | bytes 2359312 | tf_op jit(solution)/shard_map/all_gather | solution.py:69
  149.2 81.3 %all-gather.23.cloned.1.call-done = f32[3072,768]{1,0:T(8,128)} async-done(((f32[96,768]{1,0:T(8,128)}), f32[3072,768]{1,0:T(8,128)}) %all-gather.23.cloned.1.call-update) | async-done | bytes 9437200 | tf_op jit(solution)/shard_map/all_gather | solution.py:69
  230.5 84.0 %all-gather.21.cloned.1.call-done = f32[3072,768]{1,0:T(8,128)} async-done(((f32[96,768]{1,0:T(8,128)}), f32[3072,768]{1,0:T(8,128)}) %all-gather.21.cloned.1.call-update) | async-done | bytes 9437200 | tf_op jit(solution)/shard_map/all_gather | solution.py:69
  314.5 7.2 multiply_convert_fusion.1
  321.7 4.5 fusion.13
  326.2 4.8 convert_reduce_fusion
  338.4 7.9 convert_reduce_fusion.2
  346.3 9.0 multiply_reduce_fusion
  355.3 6.8 multiply_convert_fusion
  367.4 5.3 fusion.56
  381.0 4.5 copy.83
  395.2 6.2 fusion.44
  402.7 340.8 %all-reduce.7.cloned.1.call-done = (f32[4,8,72,768]{3,2,1,0:T(8,128)}, f32[4,8,24,768]{3,2,1,0:T(8,128)}, f32[4,8,96,768]{3,2,1,0:T(8,128)}, f32[4,8,96,768]{3,2,1,0:T(8,128)}) async-done(((f32[4,8,72,768]{3,2,1,0:T(8,128)}, f32[4,8,24,768]{3,2,1,0:T(8,128)}, f32[4,8,96,768]{3,2,1,0:T(8,128)}, f32[4,8,96,768]{3,2,1,0:T(8,128)}), (f32[4,8,72,768]{3,2,1,0:T(8,128)}, f32[4,8,24,768]{3,2,1,0:T(8,128)}, ...) | async-done | bytes 28311568
  752.7 7.1 fusion.24
  759.8 5.4 fusion.22
  771.5 30.8 %reduce-scatter.17.cloned.1.call-done = f32[1,1,96,768]{3,2,1,0:T(8,128)} async-done(((f32[4,1,96,768]{3,2,1,0:T(8,128)}), f32[1,1,96,768]{3,2,1,0:T(8,128)}) %reduce-scatter.17.cloned.1.call-update) | async-done | bytes 294928 | tf_op jit(solution)/shard_map/reduce_scatter | solution.py:134
  802.4 30.7 %reduce-scatter.19.cloned.1.call-done = f32[1,1,96,768]{3,2,1,0:T(8,128)} async-done(((f32[4,1,96,768]{3,2,1,0:T(8,128)}), f32[1,1,96,768]{3,2,1,0:T(8,128)}) %reduce-scatter.19.cloned.1.call-update) | async-done | bytes 294928 | tf_op jit(solution)/shard_map/reduce_scatter | solution.py:134
  833.5 42.7 %psum.7 = f32[13,768]{1,0:T(8,128)S(1)} all-reduce(f32[13,768]{1,0:T(8,128)S(1)} %concatenate.4), channel_id=1, replica_groups=mesh['wide'=8,'narrow'=4] {'wide','narrow'}, use_global_device_ids=true, to_apply=%region_22.23 | all-reduce | flops 9984 | bytes 79872 | tf_op jit(solution)/shard_map/psum | solution.py:147
  878.2 72.2 %all-gather.25.cloned.1.call-done = f32[2048,768]{1,0:T(8,128)} async-done(((f32[512,768]{1,0:T(8,128)}), f32[2048,768]{1,0:T(8,128)}) %all-gather.25.cloned.1.call-update) | async-done | bytes 6291472 | tf_op jit(solution)/shard_map/all_gather | solution.py:123
  950.4 4.9 multiply_convert_fusion.5
  955.4 110.7 %all-gather.27.cloned.1.call-done = f32[2048,768]{1,0:T(8,128)} async-done(((f32[512,768]{1,0:T(8,128)}), f32[2048,768]{1,0:T(8,128)}) %all-gather.27.cloned.1.call-update) | async-done | bytes 6291472 | tf_op jit(solution)/shard_map/all_gather | solution.py:123
  1066.0 4.9 multiply_convert_fusion.4
  1071.0 16.0 %reduce-scatter.15.cloned.1.call-done = f32[1,1,24,768]{3,2,1,0:T(8,128)} async-done(((f32[4,1,24,768]{3,2,1,0:T(8,128)}), f32[1,1,24,768]{3,2,1,0:T(8,128)}) %reduce-scatter.15.cloned.1.call-update) | async-done | bytes 73744 | tf_op jit(solution)/shard_map/reduce_scatter | solution.py:134
  1087.0 10.3 all-gather.2
  1097.3 16.3 %all-gather.29.cloned.1.call-done = f32[1,1,576,768]{3,2,1,0:T(8,128)} async-done(((f32[1,1,72,768]{3,2,1,0:T(8,128)}), f32[1,1,576,768]{3,2,1,0:T(8,128)}) %all-gather.29.cloned.1.call-update) | async-done | bytes 1769488 | tf_op jit(solution)/shard_map/all_gather | solution.py:135
  1113.5 30.9 %all-gather.31.cloned.1.call-done = f32[1,1,768,768]{3,2,1,0:T(8,128)} async-done(((f32[1,1,96,768]{3,2,1,0:T(8,128)}), f32[1,1,768,768]{3,2,1,0:T(8,128)}) %all-gather.31.cloned.1.call-update) | async-done | bytes 2359312 | tf_op jit(solution)/shard_map/all_gather | solution.py:135
  1144.5 30.8 %all-gather.33.cloned.1.call-done = f32[1,1,768,768]{3,2,1,0:T(8,128)} async-done(((f32[1,1,96,768]{3,2,1,0:T(8,128)}), f32[1,1,768,768]{3,2,1,0:T(8,128)}) %all-gather.33.cloned.1.call-update) | async-done | bytes 2359312 | tf_op jit(solution)/shard_map/all_gather | solution.py:135
  (170 shorter events, 79.0 us)
Async XLA Ops:
  7.2 21.5 %copy-start.23 = (s32[4]{0:T(128)S(1)}, s32[4]{0:T(128)}, u32[]{:S(2)}) copy-start(s32[4]{0:T(128)} %param.19) | copy-start | bytes 52
  7.2 23.6 %copy-start.21 = (f32[768]{0:T(1024)S(1)}, f32[768]{0:T(1024)}, u32[]{:S(2)}) copy-start(f32[768]{0:T(1024)} %param.30) | copy-start | bytes 9220
  7.2 36.9 %copy-start.19 = (f32[768]{0:T(1024)S(1)}, f32[768]{0:T(1024)}, u32[]{:S(2)}) copy-start(f32[768]{0:T(1024)} %param.20) | copy-start | bytes 9220
  7.2 38.4 %copy-start.12 = (bf16[2048,768]{1,0:T(8,128)(2,1)S(1)}, bf16[2048,768]{1,0:T(8,128)(2,1)}, u32[]{:S(2)}) copy-start(bf16[2048,768]{1,0:T(8,128)(2,1)} %param.17) | copy-start | bytes 9437188
  7.2 79.5 %all-gather.17.cloned.1.call-start = ((), (), s32[]{:S(2)}) async-start(), calls=%async_computation.4 | async-start | bytes 7299072 | tf_op jit(solution)/shard_map/all_gather | solution.py:69
  9.1 137.0 %all-gather.19.cloned.1.call-start = ((), (), s32[]{:S(2)}) async-start(), calls=%async_computation.5 | async-start | bytes 2433024 | tf_op jit(solution)/shard_map/all_gather | solution.py:69
  10.5 219.9 %all-gather.23.cloned.1.call-start = ((), (), s32[]{:S(2)}) async-start(), calls=%async_computation.7 | async-start | bytes 9732096 | tf_op jit(solution)/shard_map/all_gather | solution.py:69
  12.3 302.2 %all-gather.21.cloned.1.call-start = ((), (), s32[]{:S(2)}) async-start(), calls=%async_computation.6 | async-start | bytes 9732096 | tf_op jit(solution)/shard_map/all_gather | solution.py:69
  14.0 729.5 %all-reduce.7.cloned.1.call-start = ((), (), s32[]{:S(2)}) async-start(), calls=%async_computation.17 | async-start | bytes 56623104
  93.5 7.1 copy-start.7
  93.5 7.0 copy-start.16
  100.6 45.4 %copy-start.24 = (f32[768]{0:T(1024)S(1)}, f32[768]{0:T(1024)}, u32[]{:S(2)}) copy-start(f32[768]{0:T(1024)} %param.26) | copy-start | bytes 9220
  106.4 42.4 %copy-start.13 = (bf16[12,64,512]{2,1,0:T(8,128)(2,1)}, bf16[12,64,512]{2,1,0:T(8,128)(2,1)S(1)}, u32[]{:S(2)}) copy-start(bf16[12,64,512]{2,1,0:T(8,128)(2,1)S(1)} %fusion.30) | copy-start | bytes 2359300
  148.8 182.2 %copy-start.1 = (f32[512,768]{1,0:T(8,128)}, f32[512,768]{1,0:T(8,128)S(1)}, u32[]{:S(2)}) copy-start(f32[512,768]{1,0:T(8,128)S(1)} %get-tuple-element.47) | copy-start | bytes 4718596
  149.1 172.6 %copy-start.20 = (f32[768]{0:T(1024)S(1)}, f32[768]{0:T(1024)}, u32[]{:S(2)}) copy-start(f32[768]{0:T(1024)} %param.27) | copy-start | bytes 9220
  149.2 172.6 %copy-start.25 = (f32[768]{0:T(1024)S(1)}, f32[768]{0:T(1024)}, u32[]{:S(2)}) copy-start(f32[768]{0:T(1024)} %param.28) | copy-start | bytes 9220
  338.4 7.9 copy-start.17
  338.4 7.9 copy-start.18
  338.4 16.9 %slice-start = ((s8[12582912]{0:T(1024)(128)(4,1)}), s8[4194304]{0:T(1024)(128)(4,1)S(1)}, s32[]{:S(2)}) async-start(s8[12582912]{0:T(1024)(128)(4,1)} %bitcast.185), calls=%async_computation.18 | async-start | bytes 8388608
  338.4 16.9 %slice-start.1 = ((s8[12582912]{0:T(1024)(128)(4,1)}), s8[4194304]{0:T(1024)(128)(4,1)S(1)}, s32[]{:S(2)}) async-start(s8[12582912]{0:T(1024)(128)(4,1)} %bitcast.185), calls=%async_computation.19 | async-start | bytes 8388608
  346.3 9.0 slice-start.2
  355.3 6.8 copy-start.8
  374.2 6.8 copy-start.6
  401.5 369.7 %reduce-scatter.13.cloned.1.call-start = ((), (), s32[]{:S(2)}) async-start(), calls=%async_computation.10 | async-start | bytes 1105920 | tf_op jit(solution)/shard_map/reduce_scatter | solution.py:134
  746.3 56.0 %reduce-scatter.17.cloned.1.call-start = ((), (), s32[]{:S(2)}) async-start(), calls=%async_computation.12 | async-start | bytes 1474560 | tf_op jit(solution)/shard_map/reduce_scatter | solution.py:134
  749.4 83.7 %reduce-scatter.19.cloned.1.call-start = ((), (), s32[]{:S(2)}) async-start(), calls=%async_computation.13 | async-start | bytes 1474560 | tf_op jit(solution)/shard_map/reduce_scatter | solution.py:134
  752.6 197.8 %all-gather.25.cloned.1.call-start = ((), (), s32[]{:S(2)}) async-start(), calls=%async_computation.8 | async-start | bytes 7864320 | tf_op jit(solution)/shard_map/all_gather | solution.py:123
  759.7 306.3 %all-gather.27.cloned.1.call-start = ((), (), s32[]{:S(2)}) async-start(), calls=%async_computation.9 | async-start | bytes 7864320 | tf_op jit(solution)/shard_map/all_gather | solution.py:123
  768.5 318.6 %reduce-scatter.15.cloned.1.call-start = ((), (), s32[]{:S(2)}) async-start(), calls=%async_computation.11 | async-start | bytes 368640 | tf_op jit(solution)/shard_map/reduce_scatter | solution.py:134
  770.9 342.7 %all-gather.29.cloned.1.call-start = ((), (), s32[]{:S(2)}) async-start(), calls=%async_computation.14 | async-start | bytes 1990656 | tf_op jit(solution)/shard_map/all_gather | solution.py:135
  771.5 373.0 %all-gather.31.cloned.1.call-start = ((), (), s32[]{:S(2)}) async-start(), calls=%async_computation.15 | async-start | bytes 2654208 | tf_op jit(solution)/shard_map/all_gather | solution.py:135
  802.3 372.9 %all-gather.33.cloned.1.call-start = ((), (), s32[]{:S(2)}) async-start(), calls=%async_computation.16 | async-start | bytes 2654208 | tf_op jit(solution)/shard_map/all_gather | solution.py:135
  (16 other events, 41.5 us)
Sparse Core Ops, SparseCore 0:
  11.5 75.1 all-gather.16
  90.2 55.7 all-gather.18
  149.5 80.9 all-gather.22
  233.8 80.6 all-gather.20
  401.6 341.8 all-reduce.6
  746.4 24.6 reduce-scatter.12
  774.1 28.2 reduce-scatter.16
  805.2 27.8 reduce-scatter.18
  835.3 115.0 all-gather.24
  952.4 113.5 all-gather.26
  1068.9 18.0 reduce-scatter.14
  1088.8 24.7 all-gather.28
  1115.4 29.0 all-gather.30
  1146.2 29.0 all-gather.32

commit v2 on v1

v2 whole, which is shorter than its diff:
```python
import functools
import math

import jax
import jax.numpy as jnp
from jax import lax
from jax.experimental import pallas as pl
from jax.experimental.pallas import tpu as pltpu
from jax.sharding import PartitionSpec as P

HD = 64
PATCHES = 512
EPS = 1e-06
f32 = jnp.float32
bf16 = jnp.bfloat16
MESH = pl.DeviceIdType.MESH
RT = 128


def masked_rows(mask_index, mask_count, length):
    slot_ids = jnp.arange(mask_index.shape[1], dtype=jnp.int32)
    in_use = slot_ids[None, :] < mask_count[:, None]
    position = jnp.arange(length, dtype=jnp.int32)
    matches = (mask_index[:, :, None] == position[None, None, :]) & in_use[:, :, None]
    return jnp.any(matches, axis=1)


def nn(a, b):
    return lax.dot_general(a, b, (((1,), (0,)), ((), ())), preferred_element_type=f32)


def nt(a, b):
    return lax.dot_general(a, b, (((1,), (1,)), ((), ())), preferred_element_type=f32)


def tn(a, b):
    return lax.dot_general(a, b, (((0,), (0,)), ((), ())), preferred_element_type=f32)


def rds(start, size, unit=8):
    if isinstance(start, int):
        return pl.ds(start, size)
    return pl.ds(pl.multiple_of(start, unit), size)


def normalise(v):
    centred = v - jnp.mean(v, axis=-1, keepdims=True)
    inverse = lax.rsqrt(jnp.mean(centred * centred, axis=-1, keepdims=True) + EPS)
    return centred * inverse, inverse


def norm_back(upstream, xhat, inverse, gain):
    weighted = upstream * gain
    return inverse * (
        weighted
        - jnp.mean(weighted, axis=-1, keepdims=True)
        - xhat * jnp.mean(weighted * xhat, axis=-1, keepdims=True)
    )


def softmax_t(scores):
    e = jnp.exp(scores - jnp.max(scores, axis=0, keepdims=True))
    return e * (1.0 / jnp.sum(e, axis=0, keepdims=True))


class Cfg:
    pass


def make_cfg(mesh, d, t, hs):
    g = Cfg()
    g.nw, g.nz = mesh.shape["wide"], mesh.shape["narrow"]
    g.groups = g.nw // 8
    g.d, g.t, g.hs = d, t, hs
    g.pr = d // 8
    g.units = 3 * g.nz
    g.wbits = g.nw.bit_length() - 1
    g.zbits = g.nz.bit_length() - 1
    n = 0
    for name, count in (
        ("agz", 3 * g.nz), ("agx", g.units), ("agy", g.units), ("agdx", g.units), ("agdy", g.units), ("agc", g.units),
        ("rc", g.units), ("rdx", g.units), ("rdy", g.units), ("rpx", g.units), ("rpy", g.units), ("rz", 3 * g.nz),
        ("fx", 3), ("fy", 3), ("fdx", 3), ("fdy", 3), ("fc", 3), ("zb", g.nz), ("pg", g.nz), ("sm", g.wbits + g.zbits),
        ("fg", 3 * g.groups),
    ):
        setattr(g, name, n)
        n += count
    g.nsem = n
    return g


def layer_kernel(
    g,
    part, zb, mask, vecs, patches, cot_hbm,
    out, pg, ga, gb, gc, small_out, wbuf, crecv, dxr, dyr, pxr, pyr, zr, grecv,
    wq, wo, ffw, res, xh1, xh2, normed, qkv, ctx, hid, act, slope, cotv, acc, hg, bg, dqkv, r1, r2, rsb, cst, dst, pst,
    zst, zball, sm, smr, fin, ss, rs, ls,
):
    nz, d, t, hs, pr, units = g.nz, g.d, g.t, g.hs, g.pr, g.units
    half = pr // 2
    ff_units = 2 * nz
    w = lax.axis_index("wide")
    z = lax.axis_index("narrow")
    c, x, y = w % 2, (w // 2) % 2, (w // 4) % 2
    sib, xn, yn = {"wide": w + 1 - 2 * c}, {"wide": w + 2 - 4 * x}, {"wide": w + 4 - 8 * y}
    yx, yx_x, yx_y, yx_d = y * 2 + x, y * 2 + 1 - x, (1 - y) * 2 + x, (1 - y) * 2 + 1 - x
    pos, pos_x, pos_y, pos_d = c * 4 + yx, c * 4 + yx_x, c * 4 + yx_y, c * 4 + yx_d
    zp = [None] + [{"narrow": (z + k) % nz} for k in range(1, nz)]
    gp = [None] + [{"wide": (w + 8 * k) % g.nw} for k in range(1, g.groups)]
    gouts = (ga, gb, gc)

    def rcopy(src, dst, si, ri, dev):
        return pltpu.make_async_remote_copy(src, dst, ss.at[si], rs.at[ri], device_id=dev, device_id_type=MESH)

    barrier = pltpu.get_barrier_semaphore()
    partners = [sib, xn, yn] + zp[1:] + gp[1:]
    for p in partners:
        pl.semaphore_signal(barrier, inc=1, device_id=p, device_id_type=MESH)

    def row(v, i):
        return v[i : i + 1, :]

    def wrow(p, zk, q):
        return (p * nz + zk) * d + q * pr

    def ag_pk(n):
        if isinstance(n, int) and n < nz:
            return 0, n
        m = n - nz
        return 1 + m % 2, m // 2

    def own_copy(p):
        return pltpu.make_async_copy(part.at[pl.ds(p * pr, pr)], wbuf.at[rds(wrow(p, z, pos), pr)], ls.at[p])

    def ag_block(n, q, lo, size):
        p, k = ag_pk(n)
        return wbuf.at[rds(wrow(p, (z + k) % nz, q) + lo, size)]

    def ag_xy(n):
        b = ag_block(n, pos, 0, pr)
        return rcopy(b, b, g.agx + n, g.agx + n, xn), rcopy(b, b, g.agy + n, g.agy + n, yn)

    def ag_d(n):
        bx, by = ag_block(n, pos_x, 0, half), ag_block(n, pos_y, half, half)
        return rcopy(bx, bx, g.agdy + n, g.agdy + n, yn), rcopy(by, by, g.agdx + n, g.agdx + n, xn)

    def ag_c(n):
        b = ag_block(n, c * 4, 0, 4 * pr)
        return rcopy(b, b, g.agc + n, g.agc + n, sib)

    def agz(p, k):
        return rcopy(
            part.at[pl.ds(p * pr, pr)], wbuf.at[rds(wrow(p, z, pos), pr)], g.agz + p * nz + k, g.agz + p * nz + nz - k, zp[k]
        )

    def ag_s1(n):
        p, k = ag_pk(n)

        def wait_z():
            b = ag_block(n, pos, 0, pr)
            rcopy(b, b, g.agz + p * nz + k, g.agz + p * nz + k, xn).wait_recv()

        if isinstance(n, int):
            if k > 0:
                wait_z()
        else:
            pl.when(k > 0)(wait_z)
        for cp in ag_xy(n):
            cp.start()

    def ag_s2(n):
        cx, cy = ag_xy(n)
        dy, dx = ag_d(n)
        cx.wait_recv()
        dy.start()
        cy.wait_recv()
        dx.start()

    def ag_s3(n):
        dy, dx = ag_d(n)
        dy.wait_recv()
        dx.wait_recv()
        ag_c(n).start()

    def ag_conv(n):
        ag_c(n).wait_recv()
        p, k = ag_pk(n)
        zk = (z + k) % nz
        cps = [
            pltpu.make_async_copy(wbuf.at[rds(wrow(p, zk, 4 * i), 4 * pr)], cst.at[pl.ds(i * 4 * pr, 4 * pr)], ls.at[3 + i])
            for i in range(2)
        ]
        for cp in cps:
            cp.start()
        for cp in cps:
            cp.wait()
        if isinstance(n, int) and n < nz:
            for j in range(3):
                wq[j, rds(zk * hs, hs, 16), :] = cst[j * hs : (j + 1) * hs, :].astype(bf16)
            wo[rds(zk * hs, hs, 16), :] = cst[3 * hs : 4 * hs, :].astype(bf16)
        else:
            ffw[n - nz] = cst[...].astype(bf16)

    def ag_step(n):
        def run(cond, fn):
            if isinstance(cond, bool):
                if cond:
                    fn()
            else:
                pl.when(cond)(fn)

        run(n + 2 < units, lambda: ag_s1(n + 2))
        run(n < units, lambda: ag_s2(n))
        if not isinstance(n, int) or n >= 1:
            run(n - 1 < units, lambda: ag_s3(n - 1))
        if not isinstance(n, int) or n >= 2:
            run(n - 2 < units, lambda: ag_conv(n - 2))

    def ru_pk(u):
        if isinstance(u, int):
            return (2 - u % 2, u // 2) if u < ff_units else (0, u - ff_units)
        late = u // ff_units
        return (1 - late) * (2 - u % 2), (1 - late) * (u // 2) + late * (u - ff_units)

    def slot_row(u):
        return (u % 4) * d

    def sum_row(u, q):
        if isinstance(u, int):
            base = 4 * d + u * 4 * pr if u < ff_units else slot_row(u - ff_units) + c * 4 * pr
        else:
            late = u // ff_units
            base = (1 - late) * (4 * d + u * 4 * pr) + late * ((u - ff_units) * d + c * 4 * pr)
        return base + q * pr

    def rs_core(u):
        return rcopy(
            rsb.at[rds(slot_row(u) + (1 - c) * 4 * pr, 4 * pr)], crecv.at[rds(u * 4 * pr, 4 * pr)], g.rc + u, g.rc + u, sib
        )

    def rs_d(u):
        a = rcopy(rsb.at[rds(sum_row(u, yx_d), half)], dxr.at[rds(u * half, half)], g.rdx + u, g.rdx + u, xn)
        b = rcopy(rsb.at[rds(sum_row(u, yx_d) + half, half)], dyr.at[rds(u * half, half)], g.rdy + u, g.rdy + u, yn)
        return a, b

    def rs_p(u):
        a = rcopy(rsb.at[rds(sum_row(u, yx_x), pr)], pxr.at[rds(u * pr, pr)], g.rpx + u, g.rpx + u, xn)
        b = rcopy(rsb.at[rds(sum_row(u, yx_y), pr)], pyr.at[rds(u * pr, pr)], g.rpy + u, g.rpy + u, yn)
        return a, b

    def rs_z(u, dev):
        p, k = ru_pk(u)
        return rcopy(
            rsb.at[rds(sum_row(u, yx), pr)], zr.at[rds((p * nz + nz - k) * pr, pr)], g.rz + p * nz + k, g.rz + p * nz + nz - k, dev
        )

    def rs_step1(u):
        rs_core(u).wait_recv()
        cp = pltpu.make_async_copy(crecv.at[rds(u * 4 * pr, 4 * pr)], cst.at[pl.ds(0, 4 * pr)], ls.at[3])
        cp.start()
        cp.wait()
        src = slot_row(u) + c * 4 * pr
        rsb[rds(sum_row(u, 0), 4 * pr), :] = rsb[rds(src, 4 * pr), :] + cst[0 : 4 * pr, :]
        for cp in rs_d(u):
            cp.start()

    def rs_step2(u):
        a, b = rs_d(u)
        a.wait_recv()
        c0 = pltpu.make_async_copy(dxr.at[rds(u * half, half)], dst.at[pl.ds(0, half)], ls.at[3])
        c0.start()
        b.wait_recv()
        c1 = pltpu.make_async_copy(dyr.at[rds(u * half, half)], dst.at[pl.ds(half, half)], ls.at[4])
        c1.start()
        c0.wait()
        rsb[rds(sum_row(u, yx_y), half), :] += dst[0:half, :]
        c1.wait()
        rsb[rds(sum_row(u, yx_x) + half, half), :] += dst[half:pr, :]
        for cp in rs_p(u):
            cp.start()

    def rs_step3(u):
        a, b = rs_p(u)
        a.wait_recv()
        c0 = pltpu.make_async_copy(pxr.at[rds(u * pr, pr)], pst.at[pl.ds(0, pr)], ls.at[3])
        c0.start()
        b.wait_recv()
        c1 = pltpu.make_async_copy(pyr.at[rds(u * pr, pr)], pst.at[pl.ds(pr, pr)], ls.at[4])
        c1.start()
        c0.wait()
        c1.wait()
        rsb[rds(sum_row(u, yx), pr), :] += pst[0:pr, :] + pst[pr : 2 * pr, :]
        p, k = ru_pk(u)
        pl.when(k > 0)(lambda: rs_z(u, {"narrow": (z + k) % nz}).start())

    own_unit = {0: ff_units, 1: 1, 2: 0}

    def fin_xy(p):
        src = fin.at[pl.ds(p * pr, pr)]
        to = gouts[p].at[rds(pos * pr, pr)]
        return rcopy(src, to, g.fx + p, g.fx + p, xn), rcopy(src, to, g.fy + p, g.fy + p, yn)

    def fin_own(p):
        return pltpu.make_async_copy(fin.at[pl.ds(p * pr, pr)], gouts[p].at[rds(pos * pr, pr)], ls.at[5 + p])

    def fin_d(p):
        bx, by = gouts[p].at[rds(pos_x * pr, half)], gouts[p].at[rds(pos_y * pr + half, half)]
        return rcopy(bx, bx, g.fdy + p, g.fdy + p, yn), rcopy(by, by, g.fdx + p, g.fdx + p, xn)

    def fin_c(p):
        b = gouts[p].at[rds(c * 4 * pr, 4 * pr)]
        return rcopy(b, b, g.fc + p, g.fc + p, sib)

    def fin_g(p, k):
        return rcopy(
            fin.at[pl.ds(p * pr, pr)], grecv.at[pl.ds((p * g.groups + g.groups - k) * pr, pr)],
            g.fg + p * g.groups + k, g.fg + p * g.groups + g.groups - k, gp[k],
        )

    def rs_step4(p):
        total = rsb[rds(sum_row(own_unit[p], yx), pr), :]
        cps = []
        for k in range(1, nz):
            src = zr.at[pl.ds((p * nz + k) * pr, pr)]
            rcopy(src, src, g.rz + p * nz + k, g.rz + p * nz + k, xn).wait_recv()
            cps.append(pltpu.make_async_copy(src, zst.at[pl.ds((k - 1) * pr, pr)], ls.at[2 + k]))
            cps[-1].start()
        for k, cp in enumerate(cps):
            cp.wait()
            total = total + zst[k * pr : (k + 1) * pr, :]
        fin[p * pr : (p + 1) * pr, :] = total
        if g.groups > 1:
            for k in range(1, g.groups):
                fin_g(p, k).start()
            for k in range(1, g.groups):
                fin_g(p, k).wait()
            for k in range(1, g.groups):
                src = grecv.at[pl.ds((p * g.groups + k) * pr, pr)]
                cp = pltpu.make_async_copy(src, zst.at[pl.ds(0, pr)], ls.at[3])
                cp.start()
                cp.wait()
                total = total + zst[0:pr, :]
            fin[p * pr : (p + 1) * pr, :] = total
        fin_own(p).start()
        for cp in fin_xy(p):
            cp.start()

    def rs_step5(p):
        cx, cy = fin_xy(p)
        dy, dx = fin_d(p)
        cx.wait_recv()
        dy.start()
        cy.wait_recv()
        dx.start()

    def rs_step6(p):
        dy, dx = fin_d(p)
        dy.wait_recv()
        dx.wait_recv()
        fin_own(p).wait()
        fin_c(p).start()

    def sm_copy(i):
        if i < g.wbits:
            b = 1 << i
            dev = {"wide": w + b - 2 * b * ((w // b) % 2)}
        else:
            b = 1 << (i - g.wbits)
            dev = {"narrow": z + b - 2 * b * ((z // b) % 2)}
        return rcopy(sm, smr.at[pl.ds(16 * i, 16)], g.sm + i, g.sm + i, dev)

    def sm_start(i):
        sm_copy(i).start()

    def sm_finish(i):
        sm_copy(i).wait()
        sm[...] += smr[16 * i : 16 * (i + 1), :]

    def tiles(fn):
        def body(i, carry):
            fn(rds(i * RT, RT, RT))
            return carry

        lax.fori_loop(0, t // RT, body, 0)

    def load_patches(clip):
        cp = pltpu.make_async_copy(patches.at[rds(clip * t, t, 16)], bg, ls.at[8])
        cp.start()
        cp.wait()

    def first_norm(clip, keep):
        embed, gain, bias = row(vecs, 0), row(vecs, 1), row(vecs, 2)

        def fn(sl):
            m = mask[rds(clip * t + sl.start, RT), :]
            v = jnp.where(m > 0.5, embed, bg[sl, :].astype(f32))
            res[sl, :] = v
            xhat, inverse = normalise(v)
            if keep:
                xh1[sl, :] = xhat
                r1[sl, :] = inverse
            normed[sl, :] = (xhat * gain + bias).astype(bf16)

        tiles(fn)

    def project():
        biases = []
        for i in (1, 2):
            total = zball[i : i + 1, :]
            for k in range(1, nz):
                total = total + zball[8 * k + i : 8 * k + i + 1, :]
            biases.append(total)
        n = normed[...]
        qkv[0] = ((nt(n, wq[0]) + biases[0]).astype(bf16) * bf16(HD**-0.5)).astype(bf16)
        qkv[1] = nt(n, wq[1]).astype(bf16)
        qkv[2] = (nt(n, wq[2]) + biases[1]).astype(bf16)

    def head_masks():
        lane = lax.broadcasted_iota(jnp.int32, (1, 2 * HD), 1)
        first = (lane < HD).astype(f32)
        return first.astype(bf16), (1.0 - first).astype(bf16)

    def attend(i):
        sl = rds(i * 2 * HD, 2 * HD, 2 * HD)
        qp, kp, vp = qkv[0, :, sl], qkv[1, :, sl], qkv[2, :, sl]
        vt = vp.T
        outs = []
        for h, hm in enumerate(head_masks()):
            probs = softmax_t(nt(kp * hm, qp)).astype(bf16)
            outs.append(nn(vt[h * HD : (h + 1) * HD, :], probs))
        ctx[:, sl] = jnp.concatenate(outs, axis=0).T.astype(bf16)

    def attend_range(lo, hi):
        def body(i, carry):
            attend(i)
            return carry

        lax.fori_loop(lo, hi, body, 0)

    def second_norm(keep):
        acc[...] = nn(ctx[...], wo[...])
        b_out, gain, bias = row(vecs, 3), row(vecs, 4), row(vecs, 5)

        def fn(sl):
            v = res[sl, :] + acc[sl, :] + b_out
            res[sl, :] = v
            xhat, inverse = normalise(v)
            if keep:
                xh2[sl, :] = xhat
                r2[sl, :] = inverse
            hid[sl, :] = (xhat * gain + bias).astype(bf16)
            acc[sl, :] = jnp.zeros((RT, d), f32)

        tiles(fn)

    def feed(k, keep):
        bias = row(zball[rds(((z + k) % nz) * 8, 8), :], 0)
        slope[...] = nn(hid[...], ffw[2 * k])

        def fn(sl):
            v = slope[sl, :] + bias
            cdf = 0.5 * (1.0 + lax.erf(v * (0.5**0.5)))
            act[sl, :] = (v * cdf).astype(bf16)
            if keep:
                slope[sl, :] = cdf + v * jnp.exp(-0.5 * v * v) * ((0.5 / math.pi) ** 0.5)

        tiles(fn)
        acc[...] += nn(act[...], ffw[2 * k + 1])

    def write_out(clip):
        b_down = row(vecs, 6)

        def fn(sl):
            act[sl, :] = (res[sl, :] + acc[sl, :] + b_down).astype(bf16)

        tiles(fn)
        cp = pltpu.make_async_copy(act, out.at[rds(clip * t, t, 16)], ls.at[8])
        cp.start()
        cp.wait()

    def feed_back(k):
        acc2 = nt(cotv[...], ffw[2 * k + 1])
        b = (acc2 * slope[...]).astype(bf16)
        bg[...] = b
        u = 9 + (z + k) % nz
        sm[pl.ds(u, 1), :] = jnp.sum(b.astype(f32), axis=0, keepdims=True)
        part_sum = nt(bg[...], ffw[2 * k])

        @pl.when(k == 0)
        def _():
            hg[...] = part_sum

        @pl.when(k > 0)
        def _():
            hg[...] += part_sum

    zero_rows = jnp.zeros((16, d), f32)
    sm[...] = zero_rows
    cot_copy = pltpu.make_async_copy(cot_hbm.at[rds(z * t, t, 16)], cotv, ls.at[9])
    cot_copy.start()
    for p in range(3):
        own_copy(p).start()
    zball[rds(z * 8, 8), :] = zb[...]
    pl.semaphore_wait(barrier, len(partners))
    for p in range(3):
        for k in range(1, nz):
            agz(p, k).start()
    zb_copies = [
        rcopy(zb, zball.at[rds(z * 8, 8)], g.zb + k, g.zb + nz - k, zp[k]) for k in range(1, nz)
    ]
    for cp in zb_copies:
        cp.start()
    for p in range(3):
        own_copy(p).wait()
    ag_s1(0)
    ag_s1(1)
    load_patches(z)
    first_norm(z, True)
    for n in range(nz + 2):
        ag_step(n)
    for k in range(1, nz):
        rcopy(zb, zball.at[rds(((z + k) % nz) * 8, 8)], g.zb + k, g.zb + k, zp[k]).wait_recv()
    pairs = nz * hs // (2 * HD)
    project()
    ag_step(nz + 2)
    attend_range(0, pairs // 2)
    ag_step(nz + 3)
    attend_range(pairs // 2, pairs)
    second_norm(True)
    cot_copy.wait()

    def ff_body(k, carry):
        u = 2 * k

        @pl.when(k >= 2)
        def _():
            rs_core(u - 4).wait_send()
            rs_core(u - 3).wait_send()

        feed(k, True)
        rsb[rds(slot_row(u), d), :] = tn(act[...], cotv[...])
        rs_core(u).start()
        ag_step(nz + 4 + 2 * k)
        feed_back(k)
        rsb[rds(slot_row(u + 1), d), :] = tn(hid[...], bg[...])
        rs_core(u + 1).start()
        ag_step(nz + 5 + 2 * k)
        rs_step1(u)
        rs_step1(u + 1)
        return carry

    lax.fori_loop(0, nz, ff_body, 0)
    write_out(z)

    gain2 = row(vecs, 4)
    g2 = jnp.zeros((1, d), f32)

    def mid_back(i, carry):
        sg, sb, so, sc = carry
        sl = rds(i * RT, RT, RT)
        up, xhat = hg[sl, :], xh2[sl, :]
        cf = cotv[sl, :].astype(f32)
        mg = cf + norm_back(up, xhat, r2[sl, :], gain2)
        res[sl, :] = mg
        act[sl, :] = mg.astype(bf16)
        return (
            sg + jnp.sum(up * xhat, axis=0, keepdims=True),
            sb + jnp.sum(up, axis=0, keepdims=True),
            so + jnp.sum(mg, axis=0, keepdims=True),
            sc + jnp.sum(cf, axis=0, keepdims=True),
        )

    sg, sb, so, sc = lax.fori_loop(0, t // RT, mid_back, (g2, g2, g2, g2))
    sm[3:4, :], sm[4:5, :], sm[5:6, :], sm[6:7, :] = so, sg, sb, sc
    bg[...] = nt(act[...], wo[...]).astype(bf16)

    def att_back(i, carry):
        sl = rds(i * 2 * HD, 2 * HD, 2 * HD)
        qp, kp, vp, cg = qkv[0, :, sl], qkv[1, :, sl], qkv[2, :, sl], bg[:, sl]
        kt = kp.T
        masks = head_masks()
        dv = dk = None
        dq = []
        for h, hm in enumerate(masks):
            probs = softmax_t(nt(kp * hm, qp))
            dp = nt(vp * hm, cg)
            delta = jnp.sum(probs * dp, axis=0, keepdims=True)
            ds = (probs * (dp - delta)).astype(bf16)
            hf = hm.astype(f32)
            dv_h = nn(probs.astype(bf16), cg) * hf
            dk_h = nn(ds, qp) * hf
            dv = dv_h if dv is None else dv + dv_h
            dk = dk_h if dk is None else dk + dk_h
            dq.append(nn(kt[h * HD : (h + 1) * HD, :], ds))
        dqkv[0, :, sl] = (jnp.concatenate(dq, axis=0).T * (HD**-0.5)).astype(bf16)
        dqkv[1, :, sl] = dk.astype(bf16)
        dqkv[2, :, sl] = dv.astype(bf16)
        rs_step2(i)
        pl.when(i > 0)(lambda: rs_step3(i - 1))
        return carry

    lax.fori_loop(0, pairs, att_back, 0)

    for u in range(ff_units - 4, ff_units):
        rs_core(u).wait_send()
    for j in range(4):
        if j < 3:
            big = tn(dqkv[j], normed[...])
        else:
            big = tn(ctx[...], act[...])
        for zz in range(nz):
            k = (zz + nz - z) % nz
            rsb[rds(k * d + j * hs, hs), :] = big[zz * hs : (zz + 1) * hs, :]
    for u in range(ff_units, units):
        rs_core(u).start()
    acc[...] = nn(dqkv[0], wq[0]) + nn(dqkv[1], wq[1]) + nn(dqkv[2], wq[2])
    for j, r in ((0, 7), (2, 8)):
        sm[r : r + 1, :] = jnp.sum(dqkv[j].astype(f32), axis=0, keepdims=True)

    gain1 = row(vecs, 1)

    def first_back(i, carry):
        se, sg, sb = carry
        sl = rds(i * RT, RT, RT)
        up, xhat = acc[sl, :], xh1[sl, :]
        m = mask[rds(z * t + i * RT, RT), :] > 0.5
        rg = res[sl, :] + norm_back(up, xhat, r1[sl, :], gain1)
        hg[sl, :] = jnp.where(m, 0.0, rg)
        return (
            se + jnp.sum(jnp.where(m, rg, 0.0), axis=0, keepdims=True),
            sg + jnp.sum(up * xhat, axis=0, keepdims=True),
            sb + jnp.sum(up, axis=0, keepdims=True),
        )

    se, sg, sb = lax.fori_loop(0, t // RT, first_back, (g2, g2, g2))
    sm[0:1, :], sm[1:2, :], sm[2:3, :] = se, sg, sb
    pg_own = pltpu.make_async_copy(hg, pg.at[rds(z * t, t)], ls.at[9])
    pg_own.start()
    pg_copies = [rcopy(hg, pg.at[rds(z * t, t)], g.pg + k, g.pg + nz - k, zp[k]) for k in range(1, nz)]
    for cp in pg_copies:
        cp.start()
    for u in range(ff_units, units):
        rs_step1(u)

    nsm = g.wbits + g.zbits

    def service(s):
        pl.when(s + pairs < units)(lambda: rs_step2(s + pairs))
        pl.when(s + pairs - 1 < units)(lambda: rs_step3(s + pairs - 1))
        for i in range(nsm + 1):
            @pl.when(s == i)
            def _():
                if i > 0:
                    sm_finish(i - 1)
                if i < nsm:
                    sm_start(i)
        first = ff_units - pairs + 1
        for p, lead in ((2, 0), (1, 1)):
            pl.when(s == first + lead)(lambda: rs_step4(p))
            pl.when(s == first + lead + 1)(lambda: rs_step5(p))
            pl.when(s == first + lead + 2)(lambda: rs_step6(p))

    def rest(s, carry):
        clip = (z + 1 + s // 4) % nz
        seg = s % 4

        @pl.when(seg == 0)
        def _():
            load_patches(clip)
            first_norm(clip, False)
            project()

        @pl.when(seg == 1)
        def _():
            attend_range(0, pairs // 2)

        @pl.when(seg == 2)
        def _():
            attend_range(pairs // 2, pairs)
            second_norm(False)

        @pl.when(seg == 3)
        def _():
            def body(k, cc):
                feed(k, False)
                return cc

            lax.fori_loop(0, nz, body, 0)
            write_out(clip)

        service(s)
        return carry

    lax.fori_loop(0, 4 * (nz - 1), rest, 0)
    rs_step4(0)
    rs_step5(0)
    rs_step6(0)
    so_copy = pltpu.make_async_copy(sm, small_out, ls.at[9])
    pg_own.wait()
    so_copy.start()

    for cp in zb_copies:
        cp.wait_send()
    for cp in pg_copies:
        cp.wait()
    for p in range(3):
        for k in range(1, nz):
            agz(p, k).wait_send()
            u = {0: ff_units + k, 1: 2 * k + 1, 2: 2 * k}[p]
            rs_z(u, zp[k]).wait_send()
        fin_c(p).wait()
        for cp in fin_xy(p) + fin_d(p):
            cp.wait_send()
    for n in range(units):
        for cp in ag_xy(n) + ag_d(n) + (ag_c(n),) + rs_d(n) + rs_p(n):
            cp.wait_send()
    for u in range(ff_units, units):
        rs_core(u).wait_send()
    so_copy.wait()


def make(mesh):
    def on_device(
        patches, mask_index, mask_count, mask_embed, norm1_gain, norm1_bias, w_qkv, b_qv, w_out, b_out,
        norm2_gain, norm2_bias, w_up, b_up, w_down, b_down, cotangent,
    ):
        rows, d = patches.shape
        nz = mesh.shape["narrow"]
        t, hs, fs = rows // nz, w_qkv.shape[2], w_up.shape[1]
        assert t == PATCHES and fs == d and 4 * hs == d
        g = make_cfg(mesh, d, t, hs)
        pr = g.pr
        w, z = lax.axis_index("wide"), lax.axis_index("narrow")
        pos = (w % 2) * 4 + (w // 2) % 4
        first_piece = jnp.concatenate([jnp.swapaxes(w_qkv, 1, 2).reshape(3 * hs, d), w_out])
        part = jnp.concatenate(
            [lax.dynamic_slice_in_dim(a, pos * pr, pr, 0) for a in (first_piece, w_up, w_down)]
        ).astype(f32)
        zb = jnp.zeros((8, d), f32).at[0].set(b_up)
        zb = lax.dynamic_update_slice(zb, b_qv, (1, z * hs))
        mask = masked_rows(mask_index, mask_count, PATCHES).reshape(-1, 1).astype(f32)
        vecs = jnp.stack(
            [mask_embed, norm1_gain, norm1_bias, b_out, norm2_gain, norm2_bias, b_down, jnp.zeros_like(b_down)]
        )
        hbm = pl.BlockSpec(memory_space=pl.ANY)
        vm = pl.BlockSpec(memory_space=pltpu.VMEM)
        u = g.units

        def o(r, dt=f32):
            return jax.ShapeDtypeStruct((r, d), dt)

        out_shape = (
            o(rows, bf16), o(rows), o(d), o(d), o(d), o(16),
            o(u * d), o(u * 4 * pr), o(u * pr // 2), o(u * pr // 2), o(u * pr), o(u * pr), o(u * pr), o(3 * g.groups * pr),
        )
        v = pltpu.VMEM
        scratch = [
            v((3, d, d), bf16), v((d, d), bf16), v((2 * nz, d, d), bf16),
            v((t, d), f32), v((t, d), f32), v((t, d), f32), v((t, d), bf16), v((3, t, d), bf16),
            v((t, d), bf16), v((t, d), bf16), v((t, d), bf16), v((t, d), f32), v((t, d), bf16), v((t, d), f32),
            v((t, d), f32), v((t, d), bf16), v((3, t, d), bf16), v((t, 1), f32), v((t, 1), f32),
            v((4 * d + 2 * nz * 4 * pr, d), f32), v((d, d), f32), v((pr, d), f32), v((2 * pr, d), f32),
            v(((nz - 1) * pr, d), f32), v((nz * 8, d), f32), v((16, d), f32), v(((g.wbits + g.zbits) * 16, d), f32),
            v((3 * pr, d), f32),
            pltpu.SemaphoreType.DMA((g.nsem,)), pltpu.SemaphoreType.DMA((g.nsem,)), pltpu.SemaphoreType.DMA((10,)),
        ]
        outs = pl.pallas_call(
            functools.partial(layer_kernel, g),
            out_shape=out_shape,
            in_specs=[hbm, vm, vm, vm, hbm, hbm],
            out_specs=[hbm] * len(out_shape),
            scratch_shapes=scratch,
            compiler_params=pltpu.CompilerParams(
                collective_id=1, has_side_effects=True, vmem_limit_bytes=64 * 2**20 - 2**17
            ),
            name="layer",
        )(part, zb, mask, vecs, patches, cotangent)
        output, pg, ga, gb, gc, small = outs[:6]
        qkv_o = jnp.swapaxes(ga[: 3 * hs].reshape(3, hs, d), 1, 2)
        qvb = lax.dynamic_slice_in_dim(small[7:9], z * hs, hs, 1)
        upb = lax.dynamic_slice_in_dim(small[9 : 9 + nz], z, 1, 0).reshape(-1)
        return (
            output, pg.astype(bf16), small[0], small[1], small[2], qkv_o, qvb, ga[3 * hs :], small[3],
            small[4], small[5], gb, upb, gc, small[6],
        )

    return on_device


def solution(mesh):
    return jax.shard_map(
        make(mesh),
        mesh=mesh,
        in_specs=(
            P("wide", None), P("wide", None), P("wide"), P(), P(), P(), P(None, None, "narrow"), P(None, "narrow"),
            P("narrow", None), P(), P(), P(), P(None, "narrow"), P("narrow"), P("narrow", None), P(), P("wide", None),
        ),
        out_specs=(
            P("wide", None), P("wide", None), P(), P(), P(), P(None, None, "narrow"), P(None, "narrow"),
            P("narrow", None), P(), P(), P(), P(None, "narrow"), P("narrow"), P("narrow", None), P(),
        ),
        check_vma=False,
    )
```

time: 1200 us -> 527 us (0.44)
  the two profiles are of different devices: /device:TPU:0 before, /device:TPU:9 now
where the time goes in v2:
time: 527 us; the launch traced here: 525 us
  Pallas kernels  487 us (92%)
  local copies, waits for them, and re-layouts  27 us (5%)
  other arithmetic  9.68 us (2%)
    pallas_call x1, Pallas kernels, on_device(): pl.pallas_call(functools.partial(layer_kernel, g), out_shape=out_shape, i...  487 us

profile of v2, /device:TPU:9, one launch (start us, length us, event | category | flops | bytes accessed | tf_op | source)
XLA Modules:
  0.0 524.5 jit_solution(9326659866424673001)
XLA Ops:
  0.7 0.7 stack.24
  1.4 0.7 stack.25
  2.1 0.7 stack.26
  2.8 0.7 stack.27
  3.4 0.7 stack.28
  4.1 0.7 stack.29
  4.8 0.7 reshape.105
  5.5 0.7 stack.30
  6.2 0.6 stack.31.vecs
  6.9 1.8 dynamic_update_slice.3.zb
  8.7 0.0 copy-start.3
  8.7 0.7 iota_compare_fusion.1
  9.4 0.9 constant_dynamic-slice_fusion.2
  10.3 0.8 copy.33
  11.1 2.0 fusion.1
  13.2 1.1 fusion.2
  14.3 1.0 maximum_convert_fusion.part
  15.2 1.3 copy.36
  16.6 487.1 %layer.1 = (bf16[2048,768]{1,0:T(8,128)(2,1)}, f32[2048,768]{1,0:T(8,128)}, f32[768,768]{1,0:T(8,128)}, f32[768,768]{1,0:T(8,128)}, f32[768,768]{1,0:T(8,128)}, ...) custom-call(f32[288,768]{1,0:T(8,128)} %maximum_convert_fusion.part,, ...), custom_call_target="tpu_custom_call" | custom-call | tf_op jit(solution)/shard_map/layer/pallas_call | solution.py:767
  503.7 0.8 slice.51
  504.5 0.7 constant_dynamic-slice_fusion
  505.2 0.7 slice.56
  505.9 1.7 slice_reduce_fusion
  507.6 0.6 dynamic-slice_reduce_fusion
  508.2 1.9 slice.52
  510.1 2.8 slice.50
  512.9 4.9 convert_element_type.14
  517.8 1.7 copy.41
  519.5 1.1 copy-done.2
  520.6 1.4 copy.42
  522.0 1.1 copy-done.1
  523.1 1.4 copy.43
  (9 shorter events, 0.0 us)
Async XLA Ops:
  8.7 7.9 %copy-start.3 = (f32[8,768]{1,0:T(8,128)}, f32[8,768]{1,0:T(8,128)S(1)}, u32[]{:S(2)}) copy-start(f32[8,768]{1,0:T(8,128)S(1)} %dynamic_update_slice.3.zb) | copy-start | bytes 73732
  512.9 4.9 copy-start
  517.8 2.8 copy-start.2
  520.6 2.5 copy-start.1

commit v3 on v2

v3 whole, which is shorter than its diff:
```python
import functools
import math

import jax
import jax.numpy as jnp
from jax import lax
from jax.experimental import pallas as pl
from jax.experimental.pallas import tpu as pltpu
from jax.sharding import PartitionSpec as P

HD = 64
PATCHES = 512
EPS = 1e-06
f32 = jnp.float32
bf16 = jnp.bfloat16
MESH = pl.DeviceIdType.MESH
RT = 128


def nn(a, b):
    return lax.dot_general(a, b, (((1,), (0,)), ((), ())), preferred_element_type=f32)


def nt(a, b):
    return lax.dot_general(a, b, (((1,), (1,)), ((), ())), preferred_element_type=f32)


def tn(a, b):
    return lax.dot_general(a, b, (((0,), (0,)), ((), ())), preferred_element_type=f32)


def rds(start, size, unit=8):
    if isinstance(start, int):
        return pl.ds(start, size)
    return pl.ds(pl.multiple_of(start, unit), size)


def normalise(v):
    centred = v - jnp.mean(v, axis=-1, keepdims=True)
    inverse = lax.rsqrt(jnp.mean(centred * centred, axis=-1, keepdims=True) + EPS)
    return centred * inverse, inverse


def norm_back(upstream, xhat, inverse, gain):
    weighted = upstream * gain
    return inverse * (
        weighted
        - jnp.mean(weighted, axis=-1, keepdims=True)
        - xhat * jnp.mean(weighted * xhat, axis=-1, keepdims=True)
    )


def softmax_t(scores):
    e = jnp.exp(scores - jnp.max(scores, axis=0, keepdims=True))
    return e * (1.0 / jnp.sum(e, axis=0, keepdims=True))


class Cfg:
    pass


def make_cfg(mesh, d, t, hs):
    g = Cfg()
    g.nw, g.nz = mesh.shape["wide"], mesh.shape["narrow"]
    assert g.nz == 4
    g.groups = g.nw // 8
    g.d, g.t, g.hs = d, t, hs
    g.pr = d // 8
    g.units = 3 * g.nz
    g.agu = 3 * (g.nz - 1)
    g.xr = g.pr // 3
    g.wbits = g.nw.bit_length() - 1
    g.zbits = g.nz.bit_length() - 1
    g.chunks = 4
    n = 0
    for name, count in (
        ("agz", 6 * g.nz), ("age", 6 * g.nz), ("agx", g.agu), ("agy", g.agu), ("agdx", g.agu), ("agdy", g.agu), ("agc", g.agu),
        ("rc", g.units), ("rdx", g.units), ("rdy", g.units), ("rpx", g.units), ("rpy", g.units), ("rz", 6 * g.nz),
        ("fx", 3), ("fy", 3), ("fdx", 3), ("fdy", 3), ("fc", 3), ("zb", g.nz), ("pg", 2 * g.nz * g.chunks),
        ("sm", g.wbits + g.zbits), ("fg", 3 * g.groups),
    ):
        setattr(g, name, n)
        n += count
    g.nsem = n
    return g


def when(cond, fn):
    if isinstance(cond, bool):
        if cond:
            fn()
    else:
        pl.when(cond)(fn)


def layer_kernel(
    g,
    part, first_piece, w_up, w_down, zb, midx, vecs, patches, cot_hbm,
    out, pg, ga, gb, gc, small_out, wbuf, crecv, dxr, dyr, pxr, pyr, zr, grecv,
    wq, wo, ffw, res, xh1, xh2, normed, qkv, ctx, hid, act, slope, cotv, acc, hg, bg, dqkv, r1, r2, mown, rsb, cst, rst,
    dst, pst, zst, zball, sm, smr, fin, ss, rs, ls,
):
    nz, d, t, hs, pr, units = g.nz, g.d, g.t, g.hs, g.pr, g.units
    half = pr // 2
    ff_units = 2 * nz
    w = lax.axis_index("wide")
    z = lax.axis_index("narrow")
    c, x, y = w % 2, (w // 2) % 2, (w // 4) % 2
    sib, xn, yn = {"wide": w + 1 - 2 * c}, {"wide": w + 2 - 4 * x}, {"wide": w + 4 - 8 * y}
    zup, zdn = {"narrow": z + 1}, {"narrow": z - 1}
    has_up, has_dn = z < nz - 1, z > 0
    mid = (z > 0) & (z < nz - 1)
    yx, yx_x, yx_y, yx_d = y * 2 + x, y * 2 + 1 - x, (1 - y) * 2 + x, (1 - y) * 2 + 1 - x
    pos, pos_x, pos_y, pos_d = c * 4 + yx, c * 4 + yx_x, c * 4 + yx_y, c * 4 + yx_d
    zp = [None] + [{"narrow": (z + k) % nz} for k in range(1, nz)]
    gp = [None] + [{"wide": (w + 8 * k) % g.nw} for k in range(1, g.groups)]
    gouts = (ga, gb, gc)

    zside = z // 2
    zend = z + zside * (nz - 1 - 2 * z)

    def swap01(k):
        return k + zend * (1 - k // 2) * (1 - 2 * (k % 2))

    def zk(k):
        b = swap01(k)
        return b + zside * (nz - 1 - 2 * b)

    def zk_inv(zz):
        return swap01(zz + zside * (nz - 1 - 2 * zz))

    def rcopy(src, dst, si, ri, dev):
        return pltpu.make_async_remote_copy(src, dst, ss.at[si], rs.at[ri], device_id=dev, device_id_type=MESH)

    barrier = pltpu.get_barrier_semaphore()
    partners = [sib, xn, yn] + zp[1:] + gp[1:]
    for p in partners:
        pl.semaphore_signal(barrier, inc=1, device_id=p, device_id_type=MESH)

    def wrow(p, zz, q):
        return (p * nz + zz) * d + q * pr

    xr = g.xr
    hr = (pr - xr) // 2
    agu = g.agu

    def ag_pk(n):
        if isinstance(n, int) and n < nz - 1:
            return 0, n + 1
        m = n - (nz - 1)
        return 1 + m % 2, 1 + m // 2

    def own_loads():
        cps = [(first_piece.at[pl.ds(j * hs, hs)], wq.at[j, rds(z * hs, hs, 16)]) for j in range(3)]
        cps += [(first_piece.at[pl.ds(3 * hs, hs)], wo.at[rds(z * hs, hs, 16)]), (w_up, ffw.at[0]), (w_down, ffw.at[1])]
        return [pltpu.make_async_copy(src, dst, ls.at[i]) for i, (src, dst) in enumerate(cps)]

    def ag_block(n, q, lo, size):
        p, k = ag_pk(n)
        return wbuf.at[rds(wrow(p, zk(k), q) + lo, size)]

    def ag_xy(n):
        b = ag_block(n, pos, 0, pr)
        return rcopy(b, b, g.agx + n, g.agx + n, xn), rcopy(b, b, g.agy + n, g.agy + n, yn)

    def ag_d(n):
        bx, by = ag_block(n, pos_x, xr, hr), ag_block(n, pos_y, xr + hr, hr)
        return rcopy(bx, bx, g.agdy + n, g.agdy + n, yn), rcopy(by, by, g.agdx + n, g.agdx + n, xn)

    def ag_c(n):
        b = ag_block(n, c * 4, 0, 4 * pr)
        return rcopy(b, b, g.agc + n, g.agc + n, sib)

    def agz(p, zz, up, own=False):
        pair = []
        for sem, q, lo, size in ((g.agz, pos, 0, pr), (g.age, pos_d, pr, xr)):
            to = wbuf.at[rds(wrow(p, zz, q), size)]
            src = part.at[pl.ds(p * (pr + xr) + lo, size)] if own else to
            ri = sem + p * nz + zz
            pair.append(rcopy(src, to, ri + (0 if up else 3 * nz), ri, zup if up else zdn))
        return pair

    def start(cps):
        for cp in cps:
            cp.start()

    def agz_own(p):
        pl.when(has_up)(lambda: start(agz(p, z, True, True)))
        pl.when(has_dn)(lambda: start(agz(p, z, False, True)))

    def ag_z(n):
        p, k = ag_pk(n)
        zz = zk(k)

        @pl.when(mid)
        def _():
            for i, cp in enumerate(agz(p, zz, True)):
                cp.wait_recv()
                pl.when(zz < z)(lambda: agz(p, zz, True)[i].start())
                pl.when(zz > z)(lambda: agz(p, zz, False)[i].start())

    def ag_s1(n):
        p, k = ag_pk(n)
        pl.when(jnp.logical_not(mid))(lambda: agz(p, zk(k), True)[0].wait_recv())
        start(ag_xy(n))

    def ag_s2(n):
        cx, cy = ag_xy(n)
        dy, dx = ag_d(n)
        cx.wait_recv()
        dy.start()
        cy.wait_recv()
        dx.start()

    def ag_s3(n):
        p, k = ag_pk(n)
        pl.when(jnp.logical_not(mid))(lambda: agz(p, zk(k), True)[1].wait_recv())
        dy, dx = ag_d(n)
        dy.wait_recv()
        dx.wait_recv()
        ag_c(n).start()

    def ag_load(n):
        p, k = ag_pk(n)
        return [
            pltpu.make_async_copy(
                wbuf.at[rds(wrow(p, zk(k), 4 * i), 4 * pr)], cst.at[pl.ds(i * 4 * pr, 4 * pr)], ls.at[10 + i]
            )
            for i in range(2)
        ]

    def ag_conv_start(n):
        ag_c(n).wait_recv()
        start(ag_load(n))

    def ag_conv(n):
        for cp in ag_load(n):
            cp.wait()
        p, k = ag_pk(n)
        if isinstance(n, int) and n < nz - 1:
            zz = zk(k)
            for j in range(3):
                wq[j, rds(zz * hs, hs, 16), :] = cst[j * hs : (j + 1) * hs, :].astype(bf16)
            wo[rds(zz * hs, hs, 16), :] = cst[3 * hs : 4 * hs, :].astype(bf16)
        else:
            ffw[2 * k + p - 1] = cst[...].astype(bf16)

    def ag_step(n):
        static = isinstance(n, int)
        when(n < agu, lambda: ag_s2(n))
        if static:
            when(n + 2 < agu, lambda: ag_s1(n + 2))
            when(n + 3 < agu, lambda: ag_z(n + 3))
        when(n - 1 >= 0, lambda: when(n - 1 < agu, lambda: ag_s3(n - 1)))
        if not static or (n >= 2 and n != nz):
            when(n - 2 < agu, lambda: ag_conv(n - 2))
        if not static or n >= 1:
            when(n - 1 < agu, lambda: ag_conv_start(n - 1))
        if static and n == nz - 1:
            ag_conv(n - 1)

    def ru_pk(u):
        if isinstance(u, int):
            return (2 - (ff_units - 1 - u) % 2, (ff_units - 1 - u) // 2) if u < ff_units else (0, units - 1 - u)
        late = u // ff_units
        return (
            (1 - late) * (2 - (2 * ff_units - 1 - u) % 2),
            (1 - late) * ((ff_units - 1 - u + late * ff_units) // 2) + late * (units - 1 - u),
        )

    def slot_row(u):
        return ((2 * ff_units - 1 - u) % 4) * d

    def sum_row(u, q):
        if isinstance(u, int):
            base = 4 * d + u * 4 * pr if u < ff_units else slot_row(u) + c * 4 * pr
        else:
            late = u // ff_units
            base = (1 - late) * (4 * d + u * 4 * pr) + late * (slot_row(u) + c * 4 * pr)
        return base + q * pr

    def rs_core(u):
        return rcopy(
            rsb.at[rds(slot_row(u) + (1 - c) * 4 * pr, 4 * pr)], crecv.at[rds(u * 4 * pr, 4 * pr)], g.rc + u, g.rc + u, sib
        )

    def rs_d(u):
        a = rcopy(rsb.at[rds(sum_row(u, yx_d), half)], dxr.at[rds(u * half, half)], g.rdx + u, g.rdx + u, xn)
        b = rcopy(rsb.at[rds(sum_row(u, yx_d) + half, half)], dyr.at[rds(u * half, half)], g.rdy + u, g.rdy + u, yn)
        return a, b

    def rs_p(u):
        a = rcopy(rsb.at[rds(sum_row(u, yx_x), pr)], pxr.at[rds(u * pr, pr)], g.rpx + u, g.rpx + u, xn)
        b = rcopy(rsb.at[rds(sum_row(u, yx_y), pr)], pyr.at[rds(u * pr, pr)], g.rpy + u, g.rpy + u, yn)
        return a, b

    def rs_z(u, zz, up):
        p, _ = ru_pk(u)
        i = (p * nz + zz) * 2 + (0 if up else 1)
        return rcopy(rsb.at[rds(sum_row(u, yx), pr)], zr.at[rds(i * pr, pr)], g.rz + i, g.rz + i, zup if up else zdn)

    def rs_z_load(p, zz, up, slot):
        i = (p * nz + zz) * 2 + (0 if up else 1)
        src = zr.at[rds(i * pr, pr)]
        return (
            rcopy(src, src, g.rz + i, g.rz + i, sib),
            pltpu.make_async_copy(src, zst.at[pl.ds(slot * pr, pr)], ls.at[18 + slot]),
        )

    def l1(u):
        return pltpu.make_async_copy(crecv.at[rds(u * 4 * pr, 4 * pr)], rst, ls.at[12])

    def step1a(u):
        rs_core(u).wait_recv()
        l1(u).start()

    def step1b(u):
        l1(u).wait()
        src = slot_row(u) + c * 4 * pr
        rsb[rds(sum_row(u, 0), 4 * pr), :] = rsb[rds(src, 4 * pr), :] + rst[...]

    def step1c(u):
        for cp in rs_d(u):
            cp.start()

    def l2(u):
        return (
            pltpu.make_async_copy(dxr.at[rds(u * half, half)], dst.at[pl.ds(0, half)], ls.at[13]),
            pltpu.make_async_copy(dyr.at[rds(u * half, half)], dst.at[pl.ds(half, half)], ls.at[14]),
        )

    def step2a(u):
        for cp, ld in zip(rs_d(u), l2(u)):
            cp.wait_recv()
            ld.start()

    def step2b(u):
        for ld in l2(u):
            ld.wait()
        rsb[rds(sum_row(u, yx_y), half), :] += dst[0:half, :]
        rsb[rds(sum_row(u, yx_x) + half, half), :] += dst[half:pr, :]
        for cp in rs_p(u):
            cp.start()

    def l3(u):
        return (
            pltpu.make_async_copy(pxr.at[rds(u * pr, pr)], pst.at[pl.ds(0, pr)], ls.at[15]),
            pltpu.make_async_copy(pyr.at[rds(u * pr, pr)], pst.at[pl.ds(pr, pr)], ls.at[16]),
        )

    def step3a(u):
        for cp, ld in zip(rs_p(u), l3(u)):
            cp.wait_recv()
            ld.start()

    def zdir(u):
        _, k = ru_pk(u)
        zz = zk(k)
        return zz, zz > z, zz < z

    def step3b(u):
        for ld in l3(u):
            ld.wait()
        rsb[rds(sum_row(u, yx), pr), :] += pst[0:pr, :] + pst[pr : 2 * pr, :]
        zz, up, dn = zdir(u)
        pl.when(up & (z == 0))(lambda: rs_z(u, zz, True).start())
        pl.when(dn & (z == nz - 1))(lambda: rs_z(u, zz, False).start())

    def step_z(u):
        p, _ = ru_pk(u)
        zz, up, dn = zdir(u)
        for cond, flag in ((up, True), (dn, False)):
            @pl.when(cond & mid)
            def _():
                got, ld = rs_z_load(p, zz, flag, 0)
                got.wait_recv()
                ld.start()
                ld.wait()
                rsb[rds(sum_row(u, yx), pr), :] += zst[0:pr, :]
                rs_z(u, zz, flag).start()

    own_unit = {0: units - 1, 1: ff_units - 2, 2: ff_units - 1}

    def fin_xy(p):
        src = fin.at[pl.ds(p * pr, pr)]
        to = gouts[p].at[rds(pos * pr, pr)]
        return rcopy(src, to, g.fx + p, g.fx + p, xn), rcopy(src, to, g.fy + p, g.fy + p, yn)

    def fin_own(p):
        return pltpu.make_async_copy(fin.at[pl.ds(p * pr, pr)], gouts[p].at[rds(pos * pr, pr)], ls.at[5 + p])

    def fin_d(p):
        bx, by = gouts[p].at[rds(pos_x * pr, half)], gouts[p].at[rds(pos_y * pr + half, half)]
        return rcopy(bx, bx, g.fdy + p, g.fdy + p, yn), rcopy(by, by, g.fdx + p, g.fdx + p, xn)

    def fin_c(p):
        b = gouts[p].at[rds(c * 4 * pr, 4 * pr)]
        return rcopy(b, b, g.fc + p, g.fc + p, sib)

    def fin_g(p, k):
        return rcopy(
            fin.at[pl.ds(p * pr, pr)], grecv.at[pl.ds((p * g.groups + g.groups - k) * pr, pr)],
            g.fg + p * g.groups + k, g.fg + p * g.groups + g.groups - k, gp[k],
        )

    def step4(p):
        sl = slice(p * pr, (p + 1) * pr)
        fin[sl, :] = rsb[rds(sum_row(own_unit[p], yx), pr), :]
        ins = ((has_dn, True, 0), (has_up, False, 1))
        for cond, flag, slot in ins:
            @pl.when(cond)
            def _():
                got, ld = rs_z_load(p, z, flag, slot)
                got.wait_recv()
                ld.start()

        for cond, flag, slot in ins:
            @pl.when(cond)
            def _():
                rs_z_load(p, z, flag, slot)[1].wait()
                fin[sl, :] += zst[slot * pr : (slot + 1) * pr, :]

        if g.groups > 1:
            total = fin[sl, :]
            for k in range(1, g.groups):
                fin_g(p, k).start()
            for k in range(1, g.groups):
                fin_g(p, k).wait()
            for k in range(1, g.groups):
                src = grecv.at[pl.ds((p * g.groups + k) * pr, pr)]
                cp = pltpu.make_async_copy(src, zst.at[pl.ds(0, pr)], ls.at[3])
                cp.start()
                cp.wait()
                total = total + zst[0:pr, :]
            fin[sl, :] = total
        fin_own(p).start()
        for cp in fin_xy(p):
            cp.start()

    def step5(p):
        cx, cy = fin_xy(p)
        dy, dx = fin_d(p)
        cx.wait_recv()
        dy.start()
        cy.wait_recv()
        dx.start()

    def step6(p):
        dy, dx = fin_d(p)
        dy.wait_recv()
        dx.wait_recv()
        fin_own(p).wait()
        fin_c(p).start()

    def sm_copy(i):
        if i < g.wbits:
            b = 1 << i
            dev = {"wide": w + b - 2 * b * ((w // b) % 2)}
        else:
            b = 1 << (i - g.wbits)
            dev = {"narrow": z + b - 2 * b * ((z // b) % 2)}
        return rcopy(sm, smr.at[pl.ds(16 * i, 16)], g.sm + i, g.sm + i, dev)

    def sm_finish(i):
        sm_copy(i).wait()
        sm[...] += smr[16 * i : 16 * (i + 1), :]

    ck = t // g.chunks

    def pg_copy(zz, q, up):
        to = pg.at[rds(zz * t + q * ck, ck)]
        ri = g.pg + zz * g.chunks + q
        return rcopy(to, to, ri + (0 if up else nz * g.chunks), ri, zup if up else zdn)

    def pg_send(zz, q, up):
        pg_copy(zz, q, up).start()

    def pg_step(s):
        @pl.when(s < g.chunks)
        def _():
            pl.when(has_up)(lambda: pg_send(z, s, True))
            pl.when(has_dn)(lambda: pg_send(z, s, False))

        j = s - g.chunks
        for up, zz, count, more in (
            (True, z - 1 - j // g.chunks, g.chunks * z, has_up),
            (False, z + 1 + j // g.chunks, g.chunks * (nz - 1 - z), has_dn),
        ):
            @pl.when((j >= 0) & (j < count) & more)
            def _():
                pg_copy(zz, j % g.chunks, up).wait_recv()
                pg_send(zz, j % g.chunks, up)

    embed, gain1, bias1, b_out, gain2, bias2, b_down = [vecs[i : i + 1, :] for i in range(7)]

    def tiles(fn):
        def body(i, carry):
            fn(rds(i * RT, RT, RT), i * RT)
            return carry

        lax.fori_loop(0, t // RT, body, 0)

    def patches_copy(clip):
        return pltpu.make_async_copy(patches.at[rds(clip * t, t, 16)], bg, ls.at[8])

    def first_norm(clip, keep):
        listed = midx[pl.ds(clip, 1), :]

        def fn(sl, at):
            place = lax.broadcasted_iota(jnp.int32, (RT, listed.shape[1]), 0) + at
            m = jnp.max(jnp.where(listed == place, 1.0, 0.0), axis=1, keepdims=True)
            v = jnp.where(m > 0.5, embed, bg[sl, :].astype(f32))
            res[sl, :] = v
            xhat, inverse = normalise(v)
            if keep:
                mown[sl, :] = m
                xh1[sl, :] = xhat
                r1[sl, :] = inverse
            normed[sl, :] = (xhat * gain1 + bias1).astype(bf16)

        tiles(fn)

    def project():
        biases = []
        for i in (1, 2):
            total = zball[i : i + 1, :]
            for k in range(1, nz):
                total = total + zball[8 * k + i : 8 * k + i + 1, :]
            biases.append(total)
        n = normed[...]
        qkv[0] = ((nt(n, wq[0]) + biases[0]).astype(bf16) * bf16(HD**-0.5)).astype(bf16)
        qkv[1] = nt(n, wq[1]).astype(bf16)
        qkv[2] = (nt(n, wq[2]) + biases[1]).astype(bf16)

    def head_masks():
        lane = lax.broadcasted_iota(jnp.int32, (1, 2 * HD), 1)
        first = (lane < HD).astype(f32)
        return first.astype(bf16), (1.0 - first).astype(bf16)

    def attend(i):
        sl = rds(i * 2 * HD, 2 * HD, 2 * HD)
        qp, kp, vp = qkv[0, :, sl], qkv[1, :, sl], qkv[2, :, sl]
        vt = vp.T
        outs = []
        for h, hm in enumerate(head_masks()):
            probs = softmax_t(nt(kp * hm, qp)).astype(bf16)
            outs.append(nn(vt[h * HD : (h + 1) * HD, :], probs))
        ctx[:, sl] = jnp.concatenate(outs, axis=0).T.astype(bf16)

    def attend_range(lo, hi):
        def body(i, carry):
            attend(i)
            return carry

        lax.fori_loop(lo, hi, body, 0)

    def second_norm(keep):
        acc[...] = nn(ctx[...], wo[...])

        def fn(sl, at):
            v = res[sl, :] + acc[sl, :] + b_out
            res[sl, :] = v
            xhat, inverse = normalise(v)
            if keep:
                xh2[sl, :] = xhat
                r2[sl, :] = inverse
            hid[sl, :] = (xhat * gain2 + bias2).astype(bf16)
            acc[sl, :] = jnp.zeros((RT, d), f32)

        tiles(fn)

    def feed(k, keep):
        bias = zball[rds(zk(k) * 8, 8), :][0:1, :]
        slope[...] = nn(hid[...], ffw[2 * k])

        def fn(sl, at):
            v = slope[sl, :] + bias
            cdf = 0.5 * (1.0 + lax.erf(v * (0.5**0.5)))
            act[sl, :] = (v * cdf).astype(bf16)
            if keep:
                slope[sl, :] = cdf + v * jnp.exp(-0.5 * v * v) * ((0.5 / math.pi) ** 0.5)

        tiles(fn)
        acc[...] += nn(act[...], ffw[2 * k + 1])

    def write_out(clip):
        def fn(sl, at):
            act[sl, :] = (res[sl, :] + acc[sl, :] + b_down).astype(bf16)

        tiles(fn)
        cp = pltpu.make_async_copy(act, out.at[rds(clip * t, t, 16)], ls.at[8])
        cp.start()
        cp.wait()

    def feed_back(k):
        acc2 = nt(cotv[...], ffw[2 * k + 1])
        b = (acc2 * slope[...]).astype(bf16)
        bg[...] = b
        sm[pl.ds(9 + zk(k), 1), :] = jnp.sum(b.astype(f32), axis=0, keepdims=True)
        part_sum = nt(bg[...], ffw[2 * k])

        @pl.when(k == 0)
        def _():
            hg[...] = part_sum

        @pl.when(k > 0)
        def _():
            hg[...] += part_sum

    sm[...] = jnp.zeros((16, d), f32)
    cot_copy = pltpu.make_async_copy(cot_hbm.at[rds(z * t, t, 16)], cotv, ls.at[9])
    patches_copy(z).start()
    own = own_loads()
    start(own)
    cot_copy.start()
    zball[rds(z * 8, 8), :] = zb[...]
    pl.semaphore_wait(barrier, len(partners))
    agz_own(0)
    zb_copies = [
        rcopy(zb, zball.at[rds(z * 8, 8)], g.zb + k, g.zb + nz - k, zp[k]) for k in range(1, nz)
    ]
    start(zb_copies)
    patches_copy(z).wait()
    first_norm(z, True)
    ag_z(0)
    ag_s1(0)
    ag_z(1)
    pl.when(mid)(lambda: ag_s1(1))
    ag_z(2)
    agz_own(1)
    agz_own(2)
    ag_s2(0)
    pl.when(jnp.logical_not(mid))(lambda: ag_s1(1))
    ag_s1(2)
    ag_z(3)
    for n in range(1, nz):
        ag_step(n)
    for cp in own:
        cp.wait()
    for k in range(1, nz):
        rcopy(zb, zball.at[rds(((z + k) % nz) * 8, 8)], g.zb + k, g.zb + k, zp[k]).wait_recv()
    pairs = nz * hs // (2 * HD)
    project()
    for i in range(3):
        ag_step(nz + i)
        attend_range(i * pairs // 3, (i + 1) * pairs // 3)
    second_norm(True)
    cot_copy.wait()

    def ff_body(k, carry):
        ud, uu = ff_units - 1 - 2 * k, ff_units - 2 - 2 * k
        ag_step(nz + 3 + k)

        @pl.when(k >= 2)
        def _():
            rs_core(ud + 4).wait_send()
            rs_core(uu + 4).wait_send()

        pl.when(k >= 1)(lambda: step1a(ud + 2))
        feed(k, True)
        rsb[rds(slot_row(ud), d), :] = tn(act[...], cotv[...])
        rs_core(ud).start()

        @pl.when(k >= 1)
        def _():
            step1b(ud + 2)
            step1c(ud + 2)
            step1a(uu + 2)

        feed_back(k)

        @pl.when(k >= 1)
        def _():
            step1b(uu + 2)
            step1c(uu + 2)

        rsb[rds(slot_row(uu), d), :] = tn(hid[...], bg[...])
        rs_core(uu).start()
        return carry

    lax.fori_loop(0, nz, ff_body, 0)
    for u in (1, 0):
        step1a(u)
        step1b(u)
        step1c(u)
    step2a(ff_units - 1)

    none = jnp.zeros((1, d), f32)

    def mid_back(i, carry):
        sg, sb, so, sc = carry
        sl = rds(i * RT, RT, RT)
        up, xhat = hg[sl, :], xh2[sl, :]
        cf = cotv[sl, :].astype(f32)
        mg = cf + norm_back(up, xhat, r2[sl, :], gain2)
        v = res[sl, :] + acc[sl, :] + b_down
        hid[sl, :] = v.astype(bf16)
        res[sl, :] = mg
        act[sl, :] = mg.astype(bf16)
        return (
            sg + jnp.sum(up * xhat, axis=0, keepdims=True),
            sb + jnp.sum(up, axis=0, keepdims=True),
            so + jnp.sum(mg, axis=0, keepdims=True),
            sc + jnp.sum(cf, axis=0, keepdims=True),
        )

    sg, sb, so, sc = lax.fori_loop(0, t // RT, mid_back, (none, none, none, none))
    sm[3:4, :], sm[4:5, :], sm[5:6, :], sm[6:7, :] = so, sg, sb, sc
    out_own = pltpu.make_async_copy(hid, out.at[rds(z * t, t, 16)], ls.at[8])
    out_own.start()
    bg[...] = nt(act[...], wo[...]).astype(bf16)
    step2b(ff_units - 1)

    def att_back(i, carry):
        sl = rds(i * 2 * HD, 2 * HD, 2 * HD)
        qp, kp, vp, cg = qkv[0, :, sl], qkv[1, :, sl], qkv[2, :, sl], bg[:, sl]
        kt = kp.T
        masks = head_masks()
        dv = dk = None
        dq = []
        for h, hm in enumerate(masks):
            probs = softmax_t(nt(kp * hm, qp))
            dp = nt(vp * hm, cg)
            delta = jnp.sum(probs * dp, axis=0, keepdims=True)
            ds = (probs * (dp - delta)).astype(bf16)
            hf = hm.astype(f32)
            dv_h = nn(probs.astype(bf16), cg) * hf
            dk_h = nn(ds, qp) * hf
            dv = dv_h if dv is None else dv + dv_h
            dk = dk_h if dk is None else dk + dk_h
            dq.append(nn(kt[h * HD : (h + 1) * HD, :], ds))
        dqkv[0, :, sl] = (jnp.concatenate(dq, axis=0).T * (HD**-0.5)).astype(bf16)
        dqkv[1, :, sl] = dk.astype(bf16)
        dqkv[2, :, sl] = dv.astype(bf16)
        pl.when(i > 0)(lambda: step2b(i - 1))
        step2a(i)
        return carry

    lax.fori_loop(0, pairs, att_back, 0)
    acc[...] = nn(dqkv[0], wq[0]) + nn(dqkv[1], wq[1]) + nn(dqkv[2], wq[2])
    step2b(pairs - 1)

    def first_back(i, carry):
        se, sg, sb = carry
        sl = rds(i * RT, RT, RT)
        up, xhat = acc[sl, :], xh1[sl, :]
        m = mown[sl, :] > 0.5
        rg = res[sl, :] + norm_back(up, xhat, r1[sl, :], gain1)
        hg[sl, :] = jnp.where(m, 0.0, rg)
        return (
            se + jnp.sum(jnp.where(m, rg, 0.0), axis=0, keepdims=True),
            sg + jnp.sum(up * xhat, axis=0, keepdims=True),
            sb + jnp.sum(up, axis=0, keepdims=True),
        )

    se, sg, sb = lax.fori_loop(0, t // RT, first_back, (none, none, none))
    sm[0:1, :], sm[1:2, :], sm[2:3, :] = se, sg, sb
    pg_own = pltpu.make_async_copy(hg, pg.at[rds(z * t, t)], ls.at[9])
    pg_own.start()
    for j, r in ((0, 7), (2, 8)):
        sm[r : r + 1, :] = jnp.sum(dqkv[j].astype(f32), axis=0, keepdims=True)

    for u in range(4):
        rs_core(u).wait_send()
    pg_own.wait()
    pg_step(0)
    pg_step(1)
    for j in range(4):
        if j < 3:
            big = tn(dqkv[j], normed[...])
        else:
            big = tn(ctx[...], act[...])
        for zz in range(nz):
            rsb[rds(zk_inv(zz) * d + j * hs, hs), :] = big[zz * hs : (zz + 1) * hs, :]
    for u in range(ff_units, units):
        rs_core(u).start()
    out_own.wait()

    nsm = g.wbits + g.zbits
    segs = 7

    last = units - ff_units
    lead = 3

    def step2_unit(s, fn):
        when(s == 0, lambda: fn(pairs))
        when((s >= lead) & (s < lead + last), lambda: fn(ff_units - lead + s))

    def service_in(s):
        when(s < last, lambda: step1a(ff_units + s))
        step2_unit(s, step2a)
        when(s < units, lambda: step3a(s))
        when(s < units - 2, lambda: pg_step(s + 2))

    def service_out(s):
        @pl.when(s < last)
        def _():
            step1b(ff_units + s)
            step1c(ff_units + s)

        step2_unit(s, step2b)
        when(s < units, lambda: step3b(s))
        when((s >= 3) & (s < units + 3), lambda: step_z(s - 3))
        for i in range(nsm):
            when(s == 3 * i, lambda: sm_copy(i).start())
            when(s == 3 * i + 2, lambda: sm_finish(i))
        for p, at in ((1, ff_units + 2), (2, ff_units + 3), (0, units + 3)):
            when(s == at, lambda: step4(p))
            when(s == at + 1, lambda: step5(p))
            when(s == at + 2, lambda: step6(p))

    def rest(s, carry):
        clip = (z + 1 + s // segs) % nz
        seg = s % segs
        service_in(s)

        @pl.when(seg == 0)
        def _():
            patches_copy(clip).start()
            patches_copy(clip).wait()
            first_norm(clip, False)
            project()

        pl.when(seg == 1)(lambda: attend_range(0, pairs // 2))

        @pl.when(seg == 2)
        def _():
            attend_range(pairs // 2, pairs)
            second_norm(False)

        pl.when(seg >= 3)(lambda: feed(seg - 3, False))
        pl.when(seg == segs - 1)(lambda: write_out(clip))
        service_out(s)
        return carry

    lax.fori_loop(0, segs * (nz - 1), rest, 0)
    so_copy = pltpu.make_async_copy(sm, small_out, ls.at[9])
    so_copy.start()

    for cp in zb_copies:
        cp.wait_send()
    for zz in range(nz):
        for q in range(g.chunks):
            pl.when((zz != z) & jnp.logical_not(mid))(lambda: pg_copy(zz, q, True).wait_recv())
            pl.when((zz <= z) & has_up)(lambda: pg_copy(zz, q, True).wait_send())
            pl.when((zz >= z) & has_dn)(lambda: pg_copy(zz, q, False).wait_send())
        for p in range(3):
            for i in range(2):
                pl.when((zz <= z) & has_up)(lambda: agz(p, zz, True)[i].wait_send())
                pl.when((zz >= z) & has_dn)(lambda: agz(p, zz, False)[i].wait_send())
    for p in range(3):
        fin_c(p).wait()
        for cp in fin_xy(p) + fin_d(p):
            cp.wait_send()
    for n in range(agu):
        for cp in ag_xy(n) + ag_d(n) + (ag_c(n),):
            cp.wait_send()
    for n in range(units):
        for cp in rs_d(n) + rs_p(n):
            cp.wait_send()
        if ru_pk(n)[1] > 0:
            zz, up, dn = zdir(n)
            pl.when(up)(lambda: rs_z(n, zz, True).wait_send())
            pl.when(dn)(lambda: rs_z(n, zz, False).wait_send())
    for u in range(ff_units, units):
        rs_core(u).wait_send()
    so_copy.wait()


def closing_kernel(nz, hs, out_in, pg, ga, gb, gc, small, out, patch_grad, qkv_g, out_g, up_g, down_g, qv, up_b, *vectors):
    i = pl.program_id(0)
    out[...] = out_in[...]
    patch_grad[...] = pg[...].astype(bf16)
    up_g[...] = gb[...]
    down_g[...] = gc[...]
    for j in range(3):
        @pl.when(i == j)
        def _():
            qkv_g[j] = ga[j * hs : (j + 1) * hs, :].T

    @pl.when(i == 3)
    def _():
        out_g[...] = ga[3 * hs : 4 * hs, :]
        z = lax.axis_index("narrow")
        for zz in range(nz):
            @pl.when(z == zz)
            def _():
                qv[...] = small[7:9, zz * hs : (zz + 1) * hs]
                up_b[...] = small[9 + zz : 10 + zz, :]

        for k, ref in enumerate(vectors):
            ref[...] = small[k : k + 1, :]


def make(mesh):
    def on_device(
        patches, mask_index, mask_count, mask_embed, norm1_gain, norm1_bias, w_qkv, b_qv, w_out, b_out,
        norm2_gain, norm2_bias, w_up, b_up, w_down, b_down, cotangent,
    ):
        rows, d = patches.shape
        nz = mesh.shape["narrow"]
        t, hs, fs = rows // nz, w_qkv.shape[2], w_up.shape[1]
        assert t == PATCHES and fs == d and 4 * hs == d
        g = make_cfg(mesh, d, t, hs)
        pr = g.pr
        w, z = lax.axis_index("wide"), lax.axis_index("narrow")
        c, x, y = w % 2, (w // 2) % 2, (w // 4) % 2
        pos, pos_d = c * 4 + y * 2 + x, c * 4 + (1 - y) * 2 + 1 - x
        first_piece = jnp.concatenate([jnp.swapaxes(w_qkv, 1, 2).reshape(3 * hs, d), w_out])
        shares = []
        for a in (first_piece, w_up, w_down):
            shares += [lax.dynamic_slice_in_dim(a, pos * pr, pr, 0), lax.dynamic_slice_in_dim(a, pos_d * pr, g.xr, 0)]
        part = jnp.concatenate(shares).astype(f32)
        zb = jnp.zeros((8, d), f32).at[0].set(b_up)
        zb = lax.dynamic_update_slice(zb, b_qv, (1, z * hs))
        slots = jnp.arange(mask_index.shape[1], dtype=jnp.int32)
        midx = jnp.where(slots[None, :] < mask_count[:, None], mask_index, -1)
        vecs = jnp.concatenate(
            [mask_embed, norm1_gain, norm1_bias, b_out, norm2_gain, norm2_bias, b_down, b_down]
        ).reshape(8, d)
        hbm = pl.BlockSpec(memory_space=pl.ANY)
        vm = pl.BlockSpec(memory_space=pltpu.VMEM)
        u = g.units

        def o(r, dt=f32):
            return jax.ShapeDtypeStruct((r, d), dt)

        out_shape = (
            o(rows, bf16), o(rows), o(d), o(d), o(d), o(16),
            o(u * d), o(u * 4 * pr), o(u * pr // 2), o(u * pr // 2), o(u * pr), o(u * pr), o(2 * u * pr), o(3 * g.groups * pr),
        )
        v = pltpu.VMEM
        scratch = [
            v((3, d, d), bf16), v((d, d), bf16), v((2 * nz, d, d), bf16),
            v((t, d), f32), v((t, d), f32), v((t, d), f32), v((t, d), bf16), v((3, t, d), bf16),
            v((t, d), bf16), v((t, d), bf16), v((t, d), bf16), v((t, d), f32), v((t, d), bf16), v((t, d), f32),
            v((t, d), f32), v((t, d), bf16), v((3, t, d), bf16), v((t, 1), f32), v((t, 1), f32), v((t, 1), f32),
            v((4 * d + 2 * nz * 4 * pr, d), f32), v((d, d), f32), v((4 * pr, d), f32), v((pr, d), f32), v((2 * pr, d), f32),
            v((2 * pr, d), f32), v((nz * 8, d), f32), v((16, d), f32), v(((g.wbits + g.zbits) * 16, d), f32),
            v((3 * pr, d), f32),
            pltpu.SemaphoreType.DMA((g.nsem,)), pltpu.SemaphoreType.DMA((g.nsem,)), pltpu.SemaphoreType.DMA((20,)),
        ]
        outs = pl.pallas_call(
            functools.partial(layer_kernel, g),
            out_shape=out_shape,
            in_specs=[vm, hbm, hbm, hbm, vm, vm, vm, hbm, hbm],
            out_specs=[hbm] * len(out_shape),
            scratch_shapes=scratch,
            compiler_params=pltpu.CompilerParams(
                collective_id=1, has_side_effects=True, vmem_limit_bytes=64 * 2**20 - 2**17
            ),
            name="layer",
        )(
            part, first_piece, w_up, w_down, zb, midx, vecs, patches, cotangent,
        )
        steps = 8

        def cut(r):
            return pl.BlockSpec((r // steps, d), lambda i: (i, 0))

        def whole(*shape):
            return pl.BlockSpec(shape, lambda i: (0,) * len(shape))

        closed = pl.pallas_call(
            functools.partial(closing_kernel, nz, hs),
            grid=(steps,),
            out_shape=(
                o(rows, bf16), o(rows, bf16), jax.ShapeDtypeStruct((3, d, hs), f32), o(hs), o(d), o(d),
                jax.ShapeDtypeStruct((2, hs), f32), o(1),
            ) + (o(1),) * 7,
            in_specs=[cut(rows), cut(rows), whole(d, d), cut(d), cut(d), whole(16, d)],
            out_specs=(
                cut(rows), cut(rows), whole(3, d, hs), whole(hs, d), cut(d), cut(d), whole(2, hs), whole(1, d),
            ) + (whole(1, d),) * 7,
            compiler_params=pltpu.CompilerParams(vmem_limit_bytes=64 * 2**20 - 2**17),
            name="closing",
        )(*outs[:6])
        output, patch_grad, qkv_o, out_o, up_o, down_o, qvb, upb = closed[:8]
        small = [a.reshape(d) for a in closed[8:]]
        return (
            output, patch_grad, small[0], small[1], small[2], qkv_o, qvb, out_o, small[3],
            small[4], small[5], up_o, upb.reshape(d), down_o, small[6],
        )

    return on_device


def solution(mesh):
    return jax.shard_map(
        make(mesh),
        mesh=mesh,
        in_specs=(
            P("wide", None), P("wide", None), P("wide"), P(), P(), P(), P(None, None, "narrow"), P(None, "narrow"),
            P("narrow", None), P(), P(), P(), P(None, "narrow"), P("narrow"), P("narrow", None), P(), P("wide", None),
        ),
        out_specs=(
            P("wide", None), P("wide", None), P(), P(), P(), P(None, None, "narrow"), P(None, "narrow"),
            P("narrow", None), P(), P(), P(), P(None, "narrow"), P("narrow"), P("narrow", None), P(),
        ),
        check_vma=False,
    )
```

time: 527 us -> 367 us (0.70)
  the two profiles are of different devices: /device:TPU:9 before, /device:TPU:0 now
where the time goes in v3:
time: 367 us; the launch traced here: 365 us
  Pallas kernels  333 us (91%)
  other arithmetic  15.7 us (4%)
  local copies, waits for them, and re-layouts  14.8 us (4%)
    pallas_call x1, Pallas kernels, on_device(): pl.pallas_call(functools.partial(layer_kernel, g), out_shape=out_shape, i...  320 us
    pallas_call x1, Pallas kernels, on_device(): pl.pallas_call(functools.partial(closing_kernel, nz, hs), grid=(steps,),...  13.4 us
    unnamed x17, local copies, waits for them, and re-layouts  10.4 us
    pallas_call x8, other arithmetic, on_device(): pl.pallas_call(functools.partial(closing_kernel, nz, hs), grid=(steps,),...  10.3 us

profile of v3, /device:TPU:0, one launch (start us, length us, event | category | flops | bytes accessed | tf_op | source)
XLA Modules:
  0.0 364.8 jit_solution(1768911997644563509)
XLA Ops:
  0.7 0.7 reshape.90
  1.4 1.4 fusion.4.midx
  2.8 1.6 dynamic_update_slice.3.zb
  4.4 0.0 copy-start.2
  4.4 0.7 constant_dynamic-update-slice_fusion
  5.1 0.7 constant_dynamic-update-slice_fusion.7
  5.8 0.7 constant_dynamic-update-slice_fusion.6
  6.5 0.7 constant_dynamic-update-slice_fusion.5
  7.2 0.7 constant_dynamic-update-slice_fusion.4
  7.9 0.7 constant_dynamic-update-slice_fusion.3
  8.6 0.7 constant_dynamic-update-slice_fusion.2
  9.2 0.7 constant_dynamic-update-slice_fusion.1
  9.9 0.6 reshape.91.vecs
  10.6 1.1 fusion.1
  11.6 0.8 fusion.3
  12.5 0.9 dynamic-slice_dynamic-update-slice_fusion.1
  13.4 0.8 dynamic-slice_dynamic-update-slice_fusion.3
  14.2 0.9 dynamic-slice_dynamic-update-slice_fusion
  15.1 0.8 dynamic-slice_dynamic-update-slice_fusion.2
  16.0 1.1 convert_element_type.3.part
  17.1 1.1 pad_maximum_fusion.first_piece
  18.1 320.0 %layer.1 = (bf16[2048,768]{1,0:T(8,128)(2,1)}, f32[2048,768]{1,0:T(8,128)}, f32[768,768]{1,0:T(8,128)}, f32[768,768]{1,0:T(8,128)}, f32[768,768]{1,0:T(8,128)}, ...) custom-call(f32[384,768]{1,0:T(8,128)} %convert_element_type.3.part,, ...), custom_call_target="tpu_custom_call" | custom-call | tf_op jit(solution)/shard_map/layer/pallas_call | solution.py:943
  338.1 13.4 %closing.1 = (bf16[2048,768]{1,0:T(8,128)(2,1)}, bf16[2048,768]{1,0:T(8,128)(2,1)}, f32[3,768,192]{2,1,0:T(8,128)}, f32[192,768]{1,0:T(8,128)}, f32[768,768]{1,0...) custom-call(bf16[2048,768]{1,0:T(8,128)(2,1)} %get-tuple-element.48., ...), custom_call_target="tpu_custom_call" | custom-call | tf_op jit(solution)/shard_map/closing/pallas_call | solution.py:964
  351.6 1.3 reduce.2
  352.9 1.3 reduce.3
  354.1 1.3 reduce.4
  355.4 1.3 reduce.5
  356.7 1.3 reduce.6
  358.0 1.3 reduce.7
  359.3 1.3 reduce.8
  360.6 1.3 reduce.9
  361.9 2.9 copy.32
  (7 shorter events, 0.0 us)
Async XLA Ops:
  4.4 12.7 %copy-start.2 = (f32[8,768]{1,0:T(8,128)}, f32[8,768]{1,0:T(8,128)S(1)}, u32[]{:S(2)}) copy-start(f32[8,768]{1,0:T(8,128)S(1)} %dynamic_update_slice.3.zb) | copy-start | bytes 73732
  10.6 6.5 %copy-start = (bf16[3,768,192]{1,2,0:T(8,128)(2,1)S(1)}, bf16[3,768,192]{1,2,0:T(8,128)(2,1)}, u32[]{:S(2)}) copy-start(bf16[3,768,192]{1,2,0:T(8,128)(2,1)} %param.25) | copy-start | bytes 2654212
  10.6 6.5 %copy-start.1 = (bf16[192,768]{1,0:T(8,128)(2,1)S(1)}, bf16[192,768]{1,0:T(8,128)(2,1)}, u32[]{:S(2)}) copy-start(bf16[192,768]{1,0:T(8,128)(2,1)} %param.27) | copy-start | bytes 884740

commit v4 on v3

--- a/solution.py
+++ b/solution.py
@@ -95,10 +95,11 @@
 
 def layer_kernel(
     g,
-    part, first_piece, w_up, w_down, zb, midx, vecs, patches, cot_hbm,
+    qkv_t, w_out, w_up, w_down, b_up, b_qv, mask_index, mask_count, embed_ref, gain1_ref, bias1_ref, b_out_ref, gain2_ref,
+    bias2_ref, b_down_ref, patches, cot_hbm,
     out, pg, ga, gb, gc, small_out, wbuf, crecv, dxr, dyr, pxr, pyr, zr, grecv,
     wq, wo, ffw, res, xh1, xh2, normed, qkv, ctx, hid, act, slope, cotv, acc, hg, bg, dqkv, r1, r2, mown, rsb, cst, rst,
-    dst, pst, zst, zball, sm, smr, fin, ss, rs, ls,
+    zst, part, pbf, zb, zball, sm, smr, fin, ss, rs, ls,
 ):
     nz, d, t, hs, pr, units = g.nz, g.d, g.t, g.hs, g.pr, g.units
     half = pr // 2
@@ -151,8 +152,8 @@
         return 1 + m % 2, 1 + m // 2
 
     def own_loads():
-        cps = [(first_piece.at[pl.ds(j * hs, hs)], wq.at[j, rds(z * hs, hs, 16)]) for j in range(3)]
-        cps += [(first_piece.at[pl.ds(3 * hs, hs)], wo.at[rds(z * hs, hs, 16)]), (w_up, ffw.at[0]), (w_down, ffw.at[1])]
+        cps = [(qkv_t.at[pl.ds(j * hs, hs)], wq.at[j, rds(z * hs, hs, 16)]) for j in range(3)]
+        cps += [(w_out, wo.at[rds(z * hs, hs, 16)]), (w_up, ffw.at[0]), (w_down, ffw.at[1])]
         return [pltpu.make_async_copy(src, dst, ls.at[i]) for i, (src, dst) in enumerate(cps)]
 
     def ag_block(n, q, lo, size):
@@ -320,51 +321,71 @@
         rsb[rds(sum_row(u, 0), 4 * pr), :] = rsb[rds(src, 4 * pr), :] + rst[...]
 
     def step1c(u):
-        for cp in rs_d(u):
+        start(rs_d(u))
+
+    def step1(us):
+        cps = [
+            pltpu.make_async_copy(crecv.at[rds(u * 4 * pr, 4 * pr)], cst.at[pl.ds(i * 4 * pr, 4 * pr)], ls.at[36 + i])
+            for i, u in enumerate(us)
+        ]
+        for u, cp in zip(us, cps):
+            rs_core(u).wait_recv()
             cp.start()
-
-    def l2(u):
+        for i, (u, cp) in enumerate(zip(us, cps)):
+            cp.wait()
+            rsb[rds(sum_row(u, 0), 4 * pr), :] = (
+                rsb[rds(slot_row(u) + c * 4 * pr, 4 * pr), :] + cst[i * 4 * pr : (i + 1) * 4 * pr, :]
+            )
+            step1c(u)
+
+    def l2(u, i):
         return (
-            pltpu.make_async_copy(dxr.at[rds(u * half, half)], dst.at[pl.ds(0, half)], ls.at[13]),
-            pltpu.make_async_copy(dyr.at[rds(u * half, half)], dst.at[pl.ds(half, half)], ls.at[14]),
+            pltpu.make_async_copy(dxr.at[rds(u * half, half)], rst.at[pl.ds(i * pr, half)], ls.at[20 + 2 * i]),
+            pltpu.make_async_copy(dyr.at[rds(u * half, half)], rst.at[pl.ds(i * pr + half, half)], ls.at[21 + 2 * i]),
         )
 
-    def step2a(u):
-        for cp, ld in zip(rs_d(u), l2(u)):
-            cp.wait_recv()
-            ld.start()
-
-    def step2b(u):
-        for ld in l2(u):
-            ld.wait()
-        rsb[rds(sum_row(u, yx_y), half), :] += dst[0:half, :]
-        rsb[rds(sum_row(u, yx_x) + half, half), :] += dst[half:pr, :]
-        for cp in rs_p(u):
-            cp.start()
-
-    def l3(u):
+    def step2_in(us):
+        for i, u in enumerate(us):
+            for cp, ld in zip(rs_d(u), l2(u, i)):
+                cp.wait_recv()
+                ld.start()
+
+    def step2_out(us):
+        for i, u in enumerate(us):
+            for ld in l2(u, i):
+                ld.wait()
+            rsb[rds(sum_row(u, yx_y), half), :] += rst[i * pr : i * pr + half, :]
+            rsb[rds(sum_row(u, yx_x) + half, half), :] += rst[i * pr + half : (i + 1) * pr, :]
+            start(rs_p(u))
+
+    def l3(u, i):
         return (
-            pltpu.make_async_copy(pxr.at[rds(u * pr, pr)], pst.at[pl.ds(0, pr)], ls.at[15]),
-            pltpu.make_async_copy(pyr.at[rds(u * pr, pr)], pst.at[pl.ds(pr, pr)], ls.at[16]),
+            pltpu.make_async_copy(pxr.at[rds(u * pr, pr)], cst.at[pl.ds(2 * i * pr, pr)], ls.at[28 + 2 * i]),
+            pltpu.make_async_copy(pyr.at[rds(u * pr, pr)], cst.at[pl.ds((2 * i + 1) * pr, pr)], ls.at[29 + 2 * i]),
         )
-
-    def step3a(u):
-        for cp, ld in zip(rs_p(u), l3(u)):
-            cp.wait_recv()
-            ld.start()
 
     def zdir(u):
         _, k = ru_pk(u)
         zz = zk(k)
         return zz, zz > z, zz < z
 
-    def step3b(u):
-        for ld in l3(u):
-            ld.wait()
-        rsb[rds(sum_row(u, yx), pr), :] += pst[0:pr, :] + pst[pr : 2 * pr, :]
-        zz, up, dn = zdir(u)
-        pl.when(up & (z == 0))(lambda: rs_z(u, zz, True).start())
-        pl.when(dn & (z == nz - 1))(lambda: rs_z(u, zz, False).start())
+    def step3_in(us):
+        for i, u in enumerate(us):
+            for cp, ld in zip(rs_p(u), l3(u, i)):
+                cp.wait_recv()
+                ld.start()
+
+    def step3_out(us):
+        for i, u in enumerate(us):
+            for ld in l3(u, i):
+                ld.wait()
+            rsb[rds(sum_row(u, yx), pr), :] += (
+                cst[2 * i * pr : (2 * i + 1) * pr, :] + cst[(2 * i + 1) * pr : (2 * i + 2) * pr, :]
+            )
+            if ru_pk(u)[1] > 0:
+                zz, up, dn = zdir(u)
+                pl.when(up & (z == 0))(lambda: rs_z(u, zz, True).start())
+                pl.when(dn & (z == nz - 1))(lambda: rs_z(u, zz, False).start())
 
     def step_z(u):
         p, _ = ru_pk(u)
@@ -476,22 +497,24 @@
         pg_copy(zz, q, up).start()
 
     def pg_step(s):
-        @pl.when(s < g.chunks)
-        def _():
+        if s < g.chunks:
             pl.when(has_up)(lambda: pg_send(z, s, True))
             pl.when(has_dn)(lambda: pg_send(z, s, False))
-
+            return
         j = s - g.chunks
         for up, zz, count, more in (
             (True, z - 1 - j // g.chunks, g.chunks * z, has_up),
             (False, z + 1 + j // g.chunks, g.chunks * (nz - 1 - z), has_dn),
         ):
-            @pl.when((j >= 0) & (j < count) & more)
+            @pl.when((j < count) & more)
             def _():
                 pg_copy(zz, j % g.chunks, up).wait_recv()
                 pg_send(zz, j % g.chunks, up)
 
-    embed, gain1, bias1, b_out, gain2, bias2, b_down = [vecs[i : i + 1, :] for i in range(7)]
+    embed, gain1, bias1, b_out, gain2, bias2, b_down = [
+        ref[...].reshape(1, d)
+        for ref in (embed_ref, gain1_ref, bias1_ref, b_out_ref, gain2_ref, bias2_ref, b_down_ref)
+    ]
 
     def tiles(fn):
         def body(i, carry):
@@ -504,7 +527,8 @@
         return pltpu.make_async_copy(patches.at[rds(clip * t, t, 16)], bg, ls.at[8])
 
     def first_norm(clip, keep):
-        listed = midx[pl.ds(clip, 1), :]
+        slots = lax.broadcasted_iota(jnp.int32, (1, mask_index.shape[1]), 1)
+        listed = jnp.where(slots < mask_count[clip], mask_index[pl.ds(clip, 1), :], -1)
 
         def fn(sl, at):
             place = lax.broadcasted_iota(jnp.int32, (RT, listed.shape[1]), 0) + at
@@ -609,11 +633,38 @@
 
     sm[...] = jnp.zeros((16, d), f32)
     cot_copy = pltpu.make_async_copy(cot_hbm.at[rds(z * t, t, 16)], cotv, ls.at[9])
+    shares = []
+    first_rows = 3 * hs // pr
+    for p, src in enumerate((qkv_t, w_up, w_down)):
+        for q, lo, size in ((pos, 0, pr), (pos_d, pr, xr)):
+            i = len(shares)
+            to = pbf.at[pl.ds(p * (pr + xr) + lo, size)]
+
+            def share(ref, row):
+                return pltpu.make_async_copy(ref.at[rds(row, size, 16)], to, ls.at[20 + i])
+
+            if p == 0:
+                pl.when(q < first_rows)(lambda: share(qkv_t, q * pr).start())
+                pl.when(q >= first_rows)(lambda: share(w_out, (q - first_rows) * pr).start())
+                shares.append(share(w_out, 0))
+            else:
+                shares.append(share(src, q * pr))
+                shares[-1].start()
     patches_copy(z).start()
     own = own_loads()
     start(own)
     cot_copy.start()
+    zb[...] = jnp.zeros((8, d), f32)
+    zb[0:1, :] = b_up[...].reshape(1, d)
+    for zz in range(nz):
+        @pl.when(z == zz)
+        def _():
+            zb[1:3, zz * hs : (zz + 1) * hs] = b_qv[...]
+
     zball[rds(z * 8, 8), :] = zb[...]
+    for cp in shares:
+        cp.wait()
+    part[...] = pbf[...].astype(f32)
     pl.semaphore_wait(barrier, len(partners))
     agz_own(0)
     zb_copies = [
@@ -679,11 +730,8 @@
         return carry
 
     lax.fori_loop(0, nz, ff_body, 0)
-    for u in (1, 0):
-        step1a(u)
-        step1b(u)
-        step1c(u)
-    step2a(ff_units - 1)
+    step1((1, 0))
+    step2_in((3, 2))
 
     none = jnp.zeros((1, d), f32)
 
@@ -705,11 +753,11 @@
         )
 
     sg, sb, so, sc = lax.fori_loop(0, t // RT, mid_back, (none, none, none, none))
+    step2_out((3, 2))
     sm[3:4, :], sm[4:5, :], sm[5:6, :], sm[6:7, :] = so, sg, sb, sc
     out_own = pltpu.make_async_copy(hid, out.at[rds(z * t, t, 16)], ls.at[8])
     out_own.start()
     bg[...] = nt(act[...], wo[...]).astype(bf16)
-    step2b(ff_units - 1)
 
     def att_back(i, carry):
         sl = rds(i * 2 * HD, 2 * HD, 2 * HD)
@@ -732,13 +780,11 @@
         dqkv[0, :, sl] = (jnp.concatenate(dq, axis=0).T * (HD**-0.5)).astype(bf16)
         dqkv[1, :, sl] = dk.astype(bf16)
         dqkv[2, :, sl] = dv.astype(bf16)
-        pl.when(i > 0)(lambda: step2b(i - 1))
-        step2a(i)
         return carry
 
     lax.fori_loop(0, pairs, att_back, 0)
     acc[...] = nn(dqkv[0], wq[0]) + nn(dqkv[1], wq[1]) + nn(dqkv[2], wq[2])
-    step2b(pairs - 1)
+
 
     def first_back(i, carry):
         se, sg, sb = carry
@@ -760,11 +806,20 @@
     for j, r in ((0, 7), (2, 8)):
         sm[r : r + 1, :] = jnp.sum(dqkv[j].astype(f32), axis=0, keepdims=True)
 
+    nsm = g.wbits + g.zbits
+    sm_order = [0] + list(range(g.wbits, nsm)) + list(range(1, g.wbits))
+    sm_copy(sm_order[0]).start()
+
     for u in range(4):
         rs_core(u).wait_send()
+    step2_in((1, 0, 5, 4))
     pg_own.wait()
     pg_step(0)
     pg_step(1)
+    pg_step(2)
+    step2_out((1, 0, 5, 4))
+    step2_in((7, 6))
+    step2_out((7, 6))
     for j in range(4):
         if j < 3:
             big = tn(dqkv[j], normed[...])
@@ -775,44 +830,59 @@
     for u in range(ff_units, units):
         rs_core(u).start()
     out_own.wait()
-
-    nsm = g.wbits + g.zbits
+    step1((8, 9))
+    step1((10, 11))
+
     segs = 7
 
-    last = units - ff_units
-    lead = 3
-
-    def step2_unit(s, fn):
-        when(s == 0, lambda: fn(pairs))
-        when((s >= lead) & (s < lead + last), lambda: fn(ff_units - lead + s))
-
-    def service_in(s):
-        when(s < last, lambda: step1a(ff_units + s))
-        step2_unit(s, step2a)
-        when(s < units, lambda: step3a(s))
-        when(s < units - 2, lambda: pg_step(s + 2))
-
-    def service_out(s):
-        @pl.when(s < last)
-        def _():
-            step1b(ff_units + s)
-            step1c(ff_units + s)
-
-        step2_unit(s, step2b)
-        when(s < units, lambda: step3b(s))
-        when((s >= 3) & (s < units + 3), lambda: step_z(s - 3))
+    attn = tuple(range(ff_units, units))
+    plan_in = {
+        0: [lambda: step3_in((3, 2, 1, 0))],
+        2: [lambda: step3_in((5, 4, 7, 6))],
+        4: [lambda: step2_in(attn)],
+        8: [lambda: step3_in((8, 9))],
+        9: [lambda: step3_in((10, 11))],
+    }
+    plan_out = {
+        0: [lambda: step3_out((3, 2, 1, 0))],
+        2: [lambda: step3_out((5, 4, 7, 6))],
+        4: [lambda: step_z(1), lambda: step_z(0), lambda: step2_out(attn)],
+        7: [lambda: step_z(3), lambda: step_z(2)],
+        8: [lambda: step3_out((8, 9))],
+        9: [lambda: step3_out((10, 11)), lambda: step_z(5), lambda: step_z(4)],
+        11: [lambda: step_z(8)],
+        12: [lambda: step4(1), lambda: step4(2)],
+        13: [lambda: step_z(9)],
+        14: [lambda: step5(1), lambda: step5(2)],
+        15: [lambda: step_z(10)],
+        16: [lambda: step6(1), lambda: step6(2)],
+        17: [lambda: step4(0)],
+        18: [lambda: step5(0)],
+        19: [lambda: step6(0)],
+    }
+
+    def run_plan(plan, s):
+        for at, fns in plan.items():
+            @pl.when(s == at)
+            def _():
+                for fn in fns:
+                    fn()
+
+    def service(s):
+        run_plan(plan_out, s)
+        for i, at in enumerate((0, 2, 4, 5, 7, 9, 10, 12, 14)):
+            when(s == at, lambda: pg_step(i + 3))
         for i in range(nsm):
-            when(s == 3 * i, lambda: sm_copy(i).start())
-            when(s == 3 * i + 2, lambda: sm_finish(i))
-        for p, at in ((1, ff_units + 2), (2, ff_units + 3), (0, units + 3)):
-            when(s == at, lambda: step4(p))
-            when(s == at + 1, lambda: step5(p))
-            when(s == at + 2, lambda: step6(p))
+            @pl.when(s == 4 * i)
+            def _():
+                sm_finish(sm_order[i])
+                if i + 1 < nsm:
+                    sm_copy(sm_order[i + 1]).start()
 
     def rest(s, carry):
         clip = (z + 1 + s // segs) % nz
         seg = s % segs
-        service_in(s)
+        run_plan(plan_in, s)
 
         @pl.when(seg == 0)
         def _():
@@ -830,10 +900,15 @@
 
         pl.when(seg >= 3)(lambda: feed(seg - 3, False))
         pl.when(seg == segs - 1)(lambda: write_out(clip))
-        service_out(s)
+        service(s)
         return carry
 
     lax.fori_loop(0, segs * (nz - 1), rest, 0)
+    for i in range(nsm):
+        if 4 * i >= segs * (nz - 1):
+            sm_finish(sm_order[i])
+            if i + 1 < nsm:
+                sm_copy(sm_order[i + 1]).start()
     so_copy = pltpu.make_async_copy(sm, small_out, ls.at[9])
     so_copy.start()
 
@@ -876,7 +951,7 @@
     for j in range(3):
         @pl.when(i == j)
         def _():
-            qkv_g[j] = ga[j * hs : (j + 1) * hs, :].T
+            qkv_g[j] = ga[j * hs : (j + 1) * hs, :]
 
     @pl.when(i == 3)
     def _():
@@ -886,10 +961,10 @@
             @pl.when(z == zz)
             def _():
                 qv[...] = small[7:9, zz * hs : (zz + 1) * hs]
-                up_b[...] = small[9 + zz : 10 + zz, :]
+                up_b[...] = small[9 + zz : 10 + zz, :].reshape(up_b.shape)
 
         for k, ref in enumerate(vectors):
-            ref[...] = small[k : k + 1, :]
+            ref[...] = small[k : k + 1, :].reshape(ref.shape)
 
 
 def make(mesh):
@@ -903,21 +978,7 @@
         assert t == PATCHES and fs == d and 4 * hs == d
         g = make_cfg(mesh, d, t, hs)
         pr = g.pr
-        w, z = lax.axis_index("wide"), lax.axis_index("narrow")
-        c, x, y = w % 2, (w // 2) % 2, (w // 4) % 2
-        pos, pos_d = c * 4 + y * 2 + x, c * 4 + (1 - y) * 2 + 1 - x
-        first_piece = jnp.concatenate([jnp.swapaxes(w_qkv, 1, 2).reshape(3 * hs, d), w_out])
-        shares = []
-        for a in (first_piece, w_up, w_down):
-            shares += [lax.dynamic_slice_in_dim(a, pos * pr, pr, 0), lax.dynamic_slice_in_dim(a, pos_d * pr, g.xr, 0)]
-        part = jnp.concatenate(shares).astype(f32)
-        zb = jnp.zeros((8, d), f32).at[0].set(b_up)
-        zb = lax.dynamic_update_slice(zb, b_qv, (1, z * hs))
-        slots = jnp.arange(mask_index.shape[1], dtype=jnp.int32)
-        midx = jnp.where(slots[None, :] < mask_count[:, None], mask_index, -1)
-        vecs = jnp.concatenate(
-            [mask_embed, norm1_gain, norm1_bias, b_out, norm2_gain, norm2_bias, b_down, b_down]
-        ).reshape(8, d)
+        qkv_t = jnp.swapaxes(w_qkv, 1, 2).reshape(3 * hs, d)
         hbm = pl.BlockSpec(memory_space=pl.ANY)
         vm = pl.BlockSpec(memory_space=pltpu.VMEM)
         u = g.units
@@ -935,15 +996,16 @@
             v((t, d), f32), v((t, d), f32), v((t, d), f32), v((t, d), bf16), v((3, t, d), bf16),
             v((t, d), bf16), v((t, d), bf16), v((t, d), bf16), v((t, d), f32), v((t, d), bf16), v((t, d), f32),
             v((t, d), f32), v((t, d), bf16), v((3, t, d), bf16), v((t, 1), f32), v((t, 1), f32), v((t, 1), f32),
-            v((4 * d + 2 * nz * 4 * pr, d), f32), v((d, d), f32), v((4 * pr, d), f32), v((pr, d), f32), v((2 * pr, d), f32),
-            v((2 * pr, d), f32), v((nz * 8, d), f32), v((16, d), f32), v(((g.wbits + g.zbits) * 16, d), f32),
+            v((4 * d + 2 * nz * 4 * pr, d), f32), v((d, d), f32), v((4 * pr, d), f32),
+            v((2 * pr, d), f32), v((3 * (pr + g.xr), d), f32), v((3 * (pr + g.xr), d), bf16), v((8, d), f32),
+            v((nz * 8, d), f32), v((16, d), f32), v(((g.wbits + g.zbits) * 16, d), f32),
             v((3 * pr, d), f32),
-            pltpu.SemaphoreType.DMA((g.nsem,)), pltpu.SemaphoreType.DMA((g.nsem,)), pltpu.SemaphoreType.DMA((20,)),
+            pltpu.SemaphoreType.DMA((g.nsem,)), pltpu.SemaphoreType.DMA((g.nsem,)), pltpu.SemaphoreType.DMA((40,)),
         ]
         outs = pl.pallas_call(
             functools.partial(layer_kernel, g),
             out_shape=out_shape,
-            in_specs=[vm, hbm, hbm, hbm, vm, vm, vm, hbm, hbm],
+            in_specs=[hbm, hbm, hbm, hbm, vm, vm, vm, pl.BlockSpec(memory_space=pltpu.SMEM)] + [vm] * 7 + [hbm, hbm],
             out_specs=[hbm] * len(out_shape),
             scratch_shapes=scratch,
             compiler_params=pltpu.CompilerParams(
@@ -951,7 +1013,8 @@
             ),
             name="layer",
         )(
-            part, first_piece, w_up, w_down, zb, midx, vecs, patches, cotangent,
+            qkv_t, w_out, w_up, w_down, b_up, b_qv, mask_index, mask_count, mask_embed, norm1_gain, norm1_bias, b_out,
+            norm2_gain, norm2_bias, b_down, patches, cotangent,
         )
         steps = 8
 
@@ -965,21 +1028,21 @@
             functools.partial(closing_kernel, nz, hs),
             grid=(steps,),
             out_shape=(
-                o(rows, bf16), o(rows, bf16), jax.ShapeDtypeStruct((3, d, hs), f32), o(hs), o(d), o(d),
-                jax.ShapeDtypeStruct((2, hs), f32), o(1),
-            ) + (o(1),) * 7,
+                o(rows, bf16), o(rows, bf16), jax.ShapeDtypeStruct((3, hs, d), f32), o(hs), o(d), o(d),
+                jax.ShapeDtypeStruct((2, hs), f32),
+            ) + (jax.ShapeDtypeStruct((d,), f32),) * 8,
             in_specs=[cut(rows), cut(rows), whole(d, d), cut(d), cut(d), whole(16, d)],
             out_specs=(
-                cut(rows), cut(rows), whole(3, d, hs), whole(hs, d), cut(d), cut(d), whole(2, hs), whole(1, d),
-            ) + (whole(1, d),) * 7,
+                cut(rows), cut(rows), whole(3, hs, d), whole(hs, d), cut(d), cut(d), whole(2, hs),
+            ) + (whole(d),) * 8,
             compiler_params=pltpu.CompilerParams(vmem_limit_bytes=64 * 2**20 - 2**17),
             name="closing",
         )(*outs[:6])
         output, patch_grad, qkv_o, out_o, up_o, down_o, qvb, upb = closed[:8]
-        small = [a.reshape(d) for a in closed[8:]]
+        small = closed[8:]
         return (
-            output, patch_grad, small[0], small[1], small[2], qkv_o, qvb, out_o, small[3],
-            small[4], small[5], up_o, upb.reshape(d), down_o, small[6],
+            output, patch_grad, small[0], small[1], small[2], jnp.swapaxes(qkv_o, 1, 2), qvb, out_o, small[3],
+            small[4], small[5], up_o, upb, down_o, small[6],
         )
 
     return on_device

time: 367 us -> 332 us (0.905)
  other arithmetic: 15.7 us -> 0 us
  local copies, waits for them, and re-layouts: 14.8 us -> 0 us
    unnamed x17 -> x0, local copies, waits for them, and re-layouts: 10.4 us -> none
    pallas_call x8 -> x0, other arithmetic: 10.3 us -> none  [on_device(): pl.pallas_call(functools.partial(closing_kernel, nz, hs), grid=(steps,),...]
where the time goes in v4:
time: 332 us; the launch traced here: 331 us
  Pallas kernels  330 us (99%)
    pallas_call x1, Pallas kernels, on_device(): pl.pallas_call(functools.partial(layer_kernel, g), out_shape=out_shape, i...  317 us
    pallas_call x1, Pallas kernels, on_device(): pl.pallas_call(functools.partial(closing_kernel, nz, hs), grid=(steps,),...  12.8 us

profile of v4, /device:TPU:0, one launch (start us, length us, event | category | flops | bytes accessed | tf_op | source)
XLA Modules:
  0.0 330.8 jit_solution(13985831240613324096)
XLA Ops:
  0.7 317.1 %layer.1 = (bf16[2048,768]{1,0:T(8,128)(2,1)}, f32[2048,768]{1,0:T(8,128)}, f32[768,768]{1,0:T(8,128)}, f32[768,768]{1,0:T(8,128)}, f32[768,768]{1,0:T(8,128)}, ...) custom-call(bf16[576,768]{1,0:T(8,128)(2,1)} %bitcast.4, ...), custom_call_target="tpu_custom_call" | custom-call | tf_op jit(solution)/shard_map/layer/pallas_call | solution.py:1005
  317.8 12.8 %closing.1 = (bf16[2048,768]{1,0:T(8,128)(2,1)}, bf16[2048,768]{1,0:T(8,128)(2,1)}, f32[3,192,768]{2,1,0:T(8,128)}, f32[192,768]{1,0:T(8,128)}, f32[768,768]{1,0...) custom-call(bf16[2048,768]{1,0:T(8,128)(2,1)} %get-tuple-element.36., ...), custom_call_target="tpu_custom_call" | custom-call | tf_op jit(solution)/shard_map/closing/pallas_call | solution.py:1027

commit v5 on v4

--- a/solution.py
+++ b/solution.py
@@ -71,7 +71,7 @@
     g.xr = g.pr // 3
     g.wbits = g.nw.bit_length() - 1
     g.zbits = g.nz.bit_length() - 1
-    g.chunks = 4
+    g.chunks = 8
     n = 0
     for name, count in (
         ("agz", 6 * g.nz), ("age", 6 * g.nz), ("agx", g.agu), ("agy", g.agu), ("agdx", g.agu), ("agdy", g.agu), ("agc", g.agu),
@@ -607,14 +607,15 @@
         tiles(fn)
         acc[...] += nn(act[...], ffw[2 * k + 1])
 
+    def out_copy(clip):
+        return pltpu.make_async_copy(act, out.at[rds(clip * t, t, 16)], ls.at[38])
+
     def write_out(clip):
         def fn(sl, at):
             act[sl, :] = (res[sl, :] + acc[sl, :] + b_down).astype(bf16)
 
         tiles(fn)
-        cp = pltpu.make_async_copy(act, out.at[rds(clip * t, t, 16)], ls.at[8])
-        cp.start()
-        cp.wait()
+        out_copy(clip).start()
 
     def feed_back(k):
         acc2 = nt(cotv[...], ffw[2 * k + 1])
@@ -786,6 +787,8 @@
     acc[...] = nn(dqkv[0], wq[0]) + nn(dqkv[1], wq[1]) + nn(dqkv[2], wq[2])
 
 
+    step2_in((1, 0, 5, 4))
+
     def first_back(i, carry):
         se, sg, sb = carry
         sl = rds(i * RT, RT, RT)
@@ -812,15 +815,15 @@
 
     for u in range(4):
         rs_core(u).wait_send()
-    step2_in((1, 0, 5, 4))
     pg_own.wait()
     pg_step(0)
     pg_step(1)
     pg_step(2)
     step2_out((1, 0, 5, 4))
     step2_in((7, 6))
-    step2_out((7, 6))
     for j in range(4):
+        if j == 1:
+            step2_out((7, 6))
         if j < 3:
             big = tn(dqkv[j], normed[...])
         else:
@@ -830,35 +833,39 @@
     for u in range(ff_units, units):
         rs_core(u).start()
     out_own.wait()
-    step1((8, 9))
-    step1((10, 11))
+    patches_copy((z + 1) % nz).start()
 
     segs = 7
 
     attn = tuple(range(ff_units, units))
     plan_in = {
-        0: [lambda: step3_in((3, 2, 1, 0))],
-        2: [lambda: step3_in((5, 4, 7, 6))],
-        4: [lambda: step2_in(attn)],
-        8: [lambda: step3_in((8, 9))],
-        9: [lambda: step3_in((10, 11))],
+        0: [lambda: step3_in((3, 2, 1, 0)), lambda: step1a(8)],
+        1: [lambda: step1a(9)],
+        2: [lambda: step1a(10)],
+        3: [lambda: step1a(11)],
+        4: [lambda: step3_in((5, 4, 7, 6))],
+        5: [lambda: step2_in(attn)],
+        9: [lambda: step3_in((8, 9))],
+        10: [lambda: step3_in((10, 11))],
     }
     plan_out = {
-        0: [lambda: step3_out((3, 2, 1, 0))],
-        2: [lambda: step3_out((5, 4, 7, 6))],
-        4: [lambda: step_z(1), lambda: step_z(0), lambda: step2_out(attn)],
-        7: [lambda: step_z(3), lambda: step_z(2)],
-        8: [lambda: step3_out((8, 9))],
-        9: [lambda: step3_out((10, 11)), lambda: step_z(5), lambda: step_z(4)],
-        11: [lambda: step_z(8)],
-        12: [lambda: step4(1), lambda: step4(2)],
-        13: [lambda: step_z(9)],
-        14: [lambda: step5(1), lambda: step5(2)],
-        15: [lambda: step_z(10)],
-        16: [lambda: step6(1), lambda: step6(2)],
-        17: [lambda: step4(0)],
-        18: [lambda: step5(0)],
-        19: [lambda: step6(0)],
+        0: [lambda: step3_out((3, 2, 1, 0)), lambda: step1b(8), lambda: step1c(8)],
+        1: [lambda: step1b(9), lambda: step1c(9)],
+        2: [lambda: step1b(10), lambda: step1c(10)],
+        3: [lambda: step1b(11), lambda: step1c(11)],
+        4: [lambda: step3_out((5, 4, 7, 6)), lambda: step_z(1), lambda: step_z(0)],
+        5: [lambda: step2_out(attn)],
+        6: [lambda: step_z(3), lambda: step_z(2)],
+        8: [lambda: step_z(5), lambda: step_z(4)],
+        9: [lambda: step3_out((8, 9))],
+        10: [lambda: step3_out((10, 11))],
+        11: [lambda: step_z(8), lambda: step4(1), lambda: step4(2)],
+        12: [lambda: step_z(9)],
+        13: [lambda: step5(1), lambda: step5(2), lambda: step_z(10)],
+        14: [lambda: step6(1), lambda: step6(2)],
+        15: [lambda: step4(0)],
+        17: [lambda: step5(0)],
+        18: [lambda: step6(0)],
     }
 
     def run_plan(plan, s):
@@ -870,7 +877,7 @@
 
     def service(s):
         run_plan(plan_out, s)
-        for i, at in enumerate((0, 2, 4, 5, 7, 9, 10, 12, 14)):
+        for i, at in enumerate((0, 1, 2, 2, 3, 4, 5, 6, 6, 7, 8, 9, 10, 10, 11, 12, 13, 14, 15, 16, 17)):
             when(s == at, lambda: pg_step(i + 3))
         for i in range(nsm):
             @pl.when(s == 4 * i)
@@ -886,11 +893,15 @@
 
         @pl.when(seg == 0)
         def _():
-            patches_copy(clip).start()
             patches_copy(clip).wait()
             first_norm(clip, False)
             project()
 
+        @pl.when((seg == 1) & (s < segs * (nz - 2)))
+        def _():
+            patches_copy((clip + 1) % nz).start()
+
+        pl.when((seg == 1) & (s >= segs))(lambda: out_copy((clip + nz - 1) % nz).wait())
         pl.when(seg == 1)(lambda: attend_range(0, pairs // 2))
 
         @pl.when(seg == 2)
@@ -904,6 +915,7 @@
         return carry
 
     lax.fori_loop(0, segs * (nz - 1), rest, 0)
+    out_copy((z + nz - 1) % nz).wait()
     for i in range(nsm):
         if 4 * i >= segs * (nz - 1):
             sm_finish(sm_order[i])
@@ -948,14 +960,18 @@
     patch_grad[...] = pg[...].astype(bf16)
     up_g[...] = gb[...]
     down_g[...] = gc[...]
-    for j in range(3):
-        @pl.when(i == j)
-        def _():
-            qkv_g[j] = ga[j * hs : (j + 1) * hs, :]
-
-    @pl.when(i == 3)
+    first = 3 * hs // ga.shape[0]
+
+    @pl.when(i < first)
     def _():
-        out_g[...] = ga[3 * hs : 4 * hs, :]
+        qkv_g[...] = ga[...]
+
+    @pl.when(i >= first)
+    def _():
+        out_g[...] = ga[...]
+
+    @pl.when(i == 0)
+    def _():
         z = lax.axis_index("narrow")
         for zz in range(nz):
             @pl.when(z == zz)
@@ -1017,6 +1033,7 @@
             norm2_gain, norm2_bias, b_down, patches, cotangent,
         )
         steps = 8
+        first = 3 * hs * steps // d
 
         def cut(r):
             return pl.BlockSpec((r // steps, d), lambda i: (i, 0))
@@ -1028,12 +1045,15 @@
             functools.partial(closing_kernel, nz, hs),
             grid=(steps,),
             out_shape=(
-                o(rows, bf16), o(rows, bf16), jax.ShapeDtypeStruct((3, hs, d), f32), o(hs), o(d), o(d),
+                o(rows, bf16), o(rows, bf16), o(3 * hs), o(hs), o(d), o(d),
                 jax.ShapeDtypeStruct((2, hs), f32),
             ) + (jax.ShapeDtypeStruct((d,), f32),) * 8,
-            in_specs=[cut(rows), cut(rows), whole(d, d), cut(d), cut(d), whole(16, d)],
+            in_specs=[cut(rows), cut(rows), cut(d), cut(d), cut(d), whole(16, d)],
             out_specs=(
-                cut(rows), cut(rows), whole(3, hs, d), whole(hs, d), cut(d), cut(d), whole(2, hs),
+                cut(rows), cut(rows),
+                pl.BlockSpec((d // steps, d), lambda i: (jnp.minimum(i, first - 1), 0)),
+                pl.BlockSpec((d // steps, d), lambda i: (jnp.maximum(i - first, 0), 0)),
+                cut(d), cut(d), whole(2, hs),
             ) + (whole(d),) * 8,
             compiler_params=pltpu.CompilerParams(vmem_limit_bytes=64 * 2**20 - 2**17),
             name="closing",
@@ -1041,7 +1061,7 @@
         output, patch_grad, qkv_o, out_o, up_o, down_o, qvb, upb = closed[:8]
         small = closed[8:]
         return (
-            output, patch_grad, small[0], small[1], small[2], jnp.swapaxes(qkv_o, 1, 2), qvb, out_o, small[3],
+            output, patch_grad, small[0], small[1], small[2], jnp.swapaxes(qkv_o.reshape(3, hs, d), 1, 2), qvb, out_o, small[3],
             small[4], small[5], up_o, upb, down_o, small[6],
         )
 

time: 332 us -> 317 us (0.955)
  Pallas kernels: 330 us -> 315 us
    pallas_call x1, Pallas kernels: 317 us -> 303 us  [on_device(): pl.pallas_call(functools.partial(layer_kernel, g), out_shape=out_shape, i...]
where the time goes in v5:
time: 317 us; the launch traced here: 316 us
  Pallas kernels  315 us (99%)
    pallas_call x1, Pallas kernels, on_device(): pl.pallas_call(functools.partial(layer_kernel, g), out_shape=out_shape, i...  303 us
    pallas_call x1, Pallas kernels, on_device(): pl.pallas_call(functools.partial(closing_kernel, nz, hs), grid=(steps,),...  12.5 us

profile of v5, /device:TPU:0, one launch (start us, length us, event | category | flops | bytes accessed | tf_op | source)
XLA Modules:
  0.0 316.4 jit_solution(15663073415991167698)
XLA Ops:
  0.7 302.9 %layer.1 = (bf16[2048,768]{1,0:T(8,128)(2,1)}, f32[2048,768]{1,0:T(8,128)}, f32[768,768]{1,0:T(8,128)}, f32[768,768]{1,0:T(8,128)}, f32[768,768]{1,0:T(8,128)}, ...) custom-call(bf16[576,768]{1,0:T(8,128)(2,1)} %bitcast.6, ...), custom_call_target="tpu_custom_call" | custom-call | tf_op jit(solution)/shard_map/layer/pallas_call | solution.py:1021
  303.6 12.5 %closing.1 = (bf16[2048,768]{1,0:T(8,128)(2,1)}, bf16[2048,768]{1,0:T(8,128)(2,1)}, f32[576,768]{1,0:T(8,128)}, f32[192,768]{1,0:T(8,128)}, f32[768,768]{1,0:T(8...) custom-call(bf16[2048,768]{1,0:T(8,128)(2,1)} %get-tuple-element.36., ...), custom_call_target="tpu_custom_call" | custom-call | tf_op jit(solution)/shard_map/closing/pallas_call | solution.py:1044

commit v6 on v5

--- a/solution.py
+++ b/solution.py
@@ -1032,7 +1032,7 @@
             qkv_t, w_out, w_up, w_down, b_up, b_qv, mask_index, mask_count, mask_embed, norm1_gain, norm1_bias, b_out,
             norm2_gain, norm2_bias, b_down, patches, cotangent,
         )
-        steps = 8
+        steps = 4
         first = 3 * hs * steps // d
 
         def cut(r):

time: 317 us -> 315 us (level)
  no operation moved by 1% of the time
where the time goes in v6:
time: 315 us
  Pallas kernels  314 us (100%)
    pallas_call x1, Pallas kernels, on_device(): pl.pallas_call(functools.partial(layer_kernel, g), out_shape=out_shape, i...  303 us
    pallas_call x1, Pallas kernels, on_device(): pl.pallas_call(functools.partial(closing_kernel, nz, hs), grid=(steps,),...  11 us

profile of v6, /device:TPU:0, one launch (start us, length us, event | category | flops | bytes accessed | tf_op | source)
XLA Modules:
  0.0 314.8 jit_solution(7731139859651631263)
XLA Ops:
  0.7 302.9 %layer.1 = (bf16[2048,768]{1,0:T(8,128)(2,1)}, f32[2048,768]{1,0:T(8,128)}, f32[768,768]{1,0:T(8,128)}, f32[768,768]{1,0:T(8,128)}, f32[768,768]{1,0:T(8,128)}, ...) custom-call(bf16[576,768]{1,0:T(8,128)(2,1)} %bitcast.6, ...), custom_call_target="tpu_custom_call" | custom-call | tf_op jit(solution)/shard_map/layer/pallas_call | solution.py:1021
  303.6 11.0 %closing.1 = (bf16[2048,768]{1,0:T(8,128)(2,1)}, bf16[2048,768]{1,0:T(8,128)(2,1)}, f32[576,768]{1,0:T(8,128)}, f32[192,768]{1,0:T(8,128)}, f32[768,768]{1,0:T(8...) custom-call(bf16[2048,768]{1,0:T(8,128)(2,1)} %get-tuple-element.36., ...), custom_call_target="tpu_custom_call" | custom-call | tf_op jit(solution)/shard_map/closing/pallas_call | solution.py:1044
